TPU v7x, 256 devices: a whole 4x4x8 slice. The times are simulated.
256 devices in a mesh: lat: 8 (over y, x_lo), lon: 32 (over x_hi, z, core).
Axes of the slice: x: 4 (x_hi: 2, x_lo: 2; x = x_hi * 2 + x_lo), y: 4, z: 8, core: 2. Of those that a mesh axis runs over, the one named last changes fastest.
Arguments:
- features: bfloat16 [128, 512, 768], P('lat', 'lon'), may hold values from -6 to 6
- upstream: bfloat16 [128, 512, 768], P('lat', 'lon'), may hold values from -6 to 6
- attend_weight: bfloat16 [768, 2304], replicated, may hold values from -0.21875 to 0.21875
- output_weight: bfloat16 [768, 768], replicated, may hold values from -0.21875 to 0.21875
- norm_gain: float32 [768], replicated, may hold values from 0.5 to 1.5
- logit_scale: float32 [24], replicated, may hold values from 0.7 to 3.4
- table_inner: float32 [2, 512], replicated, may hold values from -4 to 4
- table_offset: float32 [512], replicated, may hold values from -0.5 to 0.5
- table_outer: float32 [512, 24], replicated, may hold values from -0.25 to 0.25
- validity: int32 [128, 512], P('lat', 'lon'), may hold values 0 or 1
Outputs:
- input_delta: bfloat16 [128, 512, 768], P('lat', 'lon')
- attend_delta: float32 [768, 2304], P('lon')
- output_delta: float32 [768, 768], P('lon')
- gain_delta: float32 [768], replicated
- scale_delta: float32 [24], replicated
- inner_delta: float32 [2, 512], replicated
- offset_delta: float32 [512], replicated
- outer_delta: float32 [512, 24], replicated
Inputs may be any that keep to these rules, and one draw needn't show every extreme that they name: `validity`: 1 marks a valid token.
All inputs are finite; a program needn't handle non-finite values. No bound on the sum of `validity` on one device may be relied on, other than what follows from the above.
Results may differ from a plain program's by a relative error of at most 0.025.
Values may be sent and summed in bfloat16 or wider, within the bound.
No kernel may reach another device: no remote copies, remote signals or barrier semaphores. Data moves between devices by JAX's collectives and lax.ppermute only.
A program may use at most 256 MiB of HBM per device.

v0:
```python
import jax
import jax.numpy as jnp
from jax import lax
from jax.sharding import PartitionSpec as P

HEADS = 24
HEAD_DIM = 32
WIN = 16
SHIFT = 8


exact_mode = lax.Precision.HIGHEST


def from_behind(value, axis, steps):
    count = lax.axis_size(axis)
    pairs = [(source, (source + steps) % count) for source in range(count)]
    return lax.ppermute(value, axis, pairs)


def offset_coords():
    spread = jnp.arange(2 * WIN - 1, dtype=jnp.float32) - (WIN - 1)
    spread = spread * (8.0 / (WIN - 1))
    spread = jnp.sign(spread) * jnp.log2(1.0 + jnp.abs(spread)) / 3.0
    first_axis = jnp.broadcast_to(spread[:, None], (2 * WIN - 1, 2 * WIN - 1))
    second = jnp.broadcast_to(spread[None, :], (2 * WIN - 1, 2 * WIN - 1))
    return jnp.stack([first_axis, second], -1).reshape(-1, 2)


def offset_pairs():
    positions = jnp.arange(WIN, dtype=jnp.int32)
    differ = positions[:, None] - positions[None, :] + WIN - 1
    onehot = (differ[:, :, None] == jnp.arange(2 * WIN - 1, dtype=jnp.int32)[None, None, :]).astype(
        jnp.float32
    )
    return onehot.reshape(WIN * WIN, 2 * WIN - 1)


def table_forward(table_inner, table_offset, table_outer):
    coords = offset_coords()
    before = jnp.dot(coords, table_inner, precision=exact_mode) + table_offset
    hidden = jnp.maximum(before, 0.0)
    logits = jnp.dot(hidden, table_outer, precision=exact_mode)
    return (coords, before, hidden, logits, 16.0 * jax.nn.sigmoid(logits))


def table_backward(grid_delta, coords, before, hidden, logits, table_outer):
    sigmoid_out = jax.nn.sigmoid(logits)
    dlogits = 16.0 * grid_delta * sigmoid_out * (1.0 - sigmoid_out)
    outer_delta = jnp.einsum("pk,ph->kh", hidden, dlogits, precision=exact_mode)
    dhidden = jnp.einsum("ph,kh->pk", dlogits, table_outer, precision=exact_mode)
    dhidden = jnp.where(before > 0.0, dhidden, 0.0)
    offset_delta = jnp.sum(dhidden, 0)
    inner_delta = jnp.einsum("pc,pk->ck", coords, dhidden, precision=exact_mode)
    return (inner_delta, offset_delta, outer_delta)


def per_device(
    features,
    upstream,
    attend_weight,
    output_weight,
    norm_gain,
    logit_scale,
    table_inner,
    table_offset,
    table_outer,
    validity,
):
    row_count, col_count, model_width = features.shape
    f32 = jnp.float32
    bf16 = jnp.bfloat16
    stacked = jnp.stack([features, upstream])
    right_strip = from_behind(stacked[:, :, :SHIFT], "lon", -1)
    widened = jnp.concatenate([stacked, right_strip], 2)
    lower_strip = from_behind(widened[:, :SHIFT], "lat", -1)
    widened = jnp.concatenate([widened, lower_strip], 1)
    rolled = widened[:, SHIFT:, SHIFT:]
    row_windows = row_count // WIN
    col_windows = col_count // WIN
    window_total = row_windows * col_windows
    token_total = row_count * col_count
    area = WIN * WIN
    span = 2 * WIN - 1

    def to_windows(grid):
        last_dims = grid.shape[2:]
        blocks = grid.reshape((row_windows, WIN, col_windows, WIN) + last_dims)
        order = (0, 2, 1, 3) + tuple(range(4, 4 + len(last_dims)))
        return jnp.transpose(blocks, order).reshape((window_total, area) + last_dims)

    tokens = to_windows(rolled[0]).reshape(token_total, model_width)
    up_tokens = to_windows(rolled[1]).reshape(token_total, model_width)
    rows_total = row_count * lax.axis_size("lat")
    global_rows = lax.axis_index("lat") * row_count + jnp.arange(row_count, dtype=jnp.int32)
    region_rows = (global_rows >= rows_total - SHIFT).astype(jnp.int32)
    region = to_windows(jnp.broadcast_to(region_rows[:, None], (row_count, col_count)))
    valid_windows = to_windows(validity)
    diagonal_mask = jnp.eye(area, dtype=bool)
    coords, before, hidden, logits, bias_grid = table_forward(
        table_inner, table_offset, table_outer
    )
    pair_table = offset_pairs()
    grid_cube = bias_grid.reshape(span, span, HEADS)
    column_part = jnp.einsum("abh,pb->hap", grid_cube, pair_table, precision=exact_mode)
    window_bias = jnp.einsum("hap,qa->hqp", column_part, pair_table, precision=exact_mode)
    window_bias = jnp.transpose(
        window_bias.reshape(HEADS, WIN, WIN, WIN, WIN), (0, 1, 3, 2, 4)
    ).reshape(HEADS, area, area)
    scale_factor = jnp.exp(logit_scale)
    projected = jnp.dot(tokens, attend_weight, preferred_element_type=f32)
    head_major = jnp.transpose(projected.reshape(window_total, area, 3 * model_width), (0, 2, 1))
    head_major = head_major.reshape(window_total, 3, HEADS, HEAD_DIM, area)
    queries = head_major[:, 0]
    key_rows = head_major[:, 1]
    value_rows = head_major[:, 2]
    query_norm = jnp.sqrt(jnp.sum(queries * queries, 2, keepdims=True) + 1.0)
    key_norm = jnp.sqrt(jnp.sum(key_rows * key_rows, 2, keepdims=True) + 1.0)
    query_unit = queries / query_norm
    key_unit = key_rows / key_norm
    query_round = (query_unit * scale_factor[None, :, None, None]).astype(bf16)
    key_round = key_unit.astype(bf16)
    value_round = value_rows.astype(bf16)

    def attention_weights(query_block, key_block, region_block, valid_block):
        allowed_block = (
            (region_block[:, None] == region_block[None, :])
            & ((valid_block[None, :] == 1) | diagonal_mask)
        ).astype(f32)
        cosines = jnp.einsum("hdi,hdj->hij", query_block, key_block, preferred_element_type=f32)
        weights = jnp.exp(cosines + window_bias) * allowed_block[None]
        return (cosines, weights / jnp.sum(weights, -1, keepdims=True))

    def forward_window(pieces):
        query_block, key_block, value_block, region_block, valid_block = pieces
        cosines, softmax_out = attention_weights(query_block, key_block, region_block, valid_block)
        mixed_heads = jnp.einsum(
            "hij,hdj->hdi", softmax_out.astype(bf16), value_block, preferred_element_type=f32
        )
        return mixed_heads.astype(bf16)

    heads_major = lax.map(
        forward_window, (query_round, key_round, value_round, region, valid_windows)
    )
    heads_out = jnp.transpose(
        heads_major.reshape(window_total, model_width, area), (0, 2, 1)
    ).reshape(token_total, model_width)
    mixed_out = jnp.dot(heads_out, output_weight, preferred_element_type=f32)
    centre = jnp.mean(mixed_out, -1, keepdims=True)
    variance = jnp.mean((mixed_out - centre) ** 2, -1, keepdims=True)
    inverse = 1.0 / jnp.sqrt(variance + 1e-05)
    normed = (mixed_out - centre) * inverse
    up_float = up_tokens.astype(f32)
    dnormed = up_float * norm_gain
    dmixed = (
        dnormed
        - jnp.mean(dnormed, -1, keepdims=True)
        - normed * jnp.mean(dnormed * normed, -1, keepdims=True)
    ) * inverse
    dmixed = dmixed.astype(bf16)
    dheads = jnp.einsum("tc,dc->td", dmixed, output_weight, preferred_element_type=f32).astype(bf16)

    def reduce_offsets(dscores):
        cube = jnp.transpose(dscores.reshape(HEADS, WIN, WIN, WIN, WIN), (0, 1, 3, 2, 4))
        column_sum = jnp.dot(cube.reshape(HEADS * area, area), pair_table, precision=exact_mode)
        return jnp.einsum(
            "hpb,pa->abh", column_sum.reshape(HEADS, area, span), pair_table, precision=exact_mode
        )

    def backward_window(running, pieces):
        scale_sum, table_sum = running
        query_block, key_block, value_block, region_block, valid_block, dheads_block = pieces
        cosines, softmax_out = attention_weights(query_block, key_block, region_block, valid_block)
        dprobs = jnp.einsum("hdi,hdj->hij", dheads_block, value_block, preferred_element_type=f32)
        dscores = softmax_out * (dprobs - jnp.sum(softmax_out * dprobs, -1, keepdims=True))
        value_delta = jnp.einsum(
            "hij,hdi->hdj", softmax_out.astype(bf16), dheads_block, preferred_element_type=f32
        )
        dscores_round = dscores.astype(bf16)
        query_grad = jnp.einsum(
            "hij,hdj->hdi", dscores_round, key_block, preferred_element_type=f32
        )
        key_grad = jnp.einsum(
            "hij,hdi->hdj", dscores_round, query_block, preferred_element_type=f32
        )
        scale_sum = scale_sum + jnp.sum(dscores * cosines, (1, 2))
        table_sum = table_sum + reduce_offsets(dscores)
        return ((scale_sum, table_sum), (query_grad, key_grad, value_delta))

    start_state = (jnp.zeros((HEADS,), f32), jnp.zeros((span, span, HEADS), f32))
    dheads_major = jnp.transpose(dheads.reshape(window_total, area, model_width), (0, 2, 1))
    dheads_major = dheads_major.reshape(window_total, HEADS, HEAD_DIM, area)
    final_state, grads_out = lax.scan(
        backward_window,
        start_state,
        (query_round, key_round, value_round, region, valid_windows, dheads_major),
    )
    scale_sum, table_part = final_state
    query_grad = grads_out[0] * scale_factor[None, :, None, None]
    key_grad = grads_out[1]
    value_delta = grads_out[2]
    query_delta = (
        query_grad - query_unit * jnp.sum(query_unit * query_grad, 2, keepdims=True)
    ) / query_norm
    key_delta = (key_grad - key_unit * jnp.sum(key_unit * key_grad, 2, keepdims=True)) / key_norm
    delta_major = jnp.stack([query_delta, key_delta, value_delta], 1).reshape(
        window_total, 3 * model_width, area
    )
    dprojected = (
        jnp.transpose(delta_major, (0, 2, 1)).reshape(token_total, 3 * model_width).astype(bf16)
    )
    dtokens = (
        up_float + jnp.einsum("te,de->td", dprojected, attend_weight, preferred_element_type=f32)
    ).astype(bf16)
    both_part = lax.psum_scatter(
        jnp.concatenate(
            [
                jnp.einsum("tr,tc->rc", tokens, dprojected, preferred_element_type=f32),
                jnp.einsum("tr,tc->rc", heads_out, dmixed, preferred_element_type=f32),
            ],
            1,
        ).astype(jnp.bfloat16),
        "lon",
        scatter_dimension=0,
        tiled=True,
    )
    both_total = lax.psum(both_part, "lat").astype(jnp.float32)
    attend_delta = both_total[:, : 3 * model_width]
    output_delta = both_total[:, 3 * model_width :]
    dgrid = dtokens.reshape(row_windows, col_windows, WIN, WIN, model_width)
    dgrid = jnp.transpose(dgrid, (0, 2, 1, 3, 4)).reshape(row_count, col_count, model_width)
    left_strip = from_behind(dgrid[:, col_count - SHIFT :], "lon", 1)
    spread_grid = jnp.concatenate([left_strip, dgrid], 1)
    upper_strip = from_behind(spread_grid[row_count - SHIFT :], "lat", 1)
    spread_grid = jnp.concatenate([upper_strip, spread_grid], 0)
    input_delta = spread_grid[:row_count, :col_count]
    gain_part = jnp.sum(up_float * normed, 0)
    gain_delta, scale_delta, table_total = lax.psum(
        (gain_part, scale_sum, table_part), ("lat", "lon")
    )
    grid_delta = table_total.reshape(-1, HEADS)
    inner_delta, offset_delta, outer_delta = table_backward(
        grid_delta, coords, before, hidden, logits, table_outer
    )
    return (
        input_delta,
        attend_delta,
        output_delta,
        gain_delta,
        scale_delta,
        inner_delta,
        offset_delta,
        outer_delta,
    )


def solution(mesh):
    in_specs = (
        P("lat", "lon", None),
        P("lat", "lon", None),
        P(),
        P(),
        P(),
        P(),
        P(),
        P(),
        P(),
        P("lat", "lon"),
    )
    out_specs = (P("lat", "lon", None), P("lon", None), P("lon", None), P(), P(), P(), P(), P())
    return jax.shard_map(
        per_device, mesh=mesh, in_specs=in_specs, out_specs=out_specs, check_vma=False
    )
```

profile of v0, /device:TPU:2, one launch (start us, length us, event | category | flops | bytes accessed | tf_op | source)
XLA Modules:
  0.0 696.0 jit_solution(1908414394108960138)
XLA Ops:
  8.1 1.9 pad_maximum_fusion.9
  10.0 6.9 collective-permute-start
  16.9 1.3 broadcast_compare_fusion
  18.9 0.9 reshape.286
  19.7 2.5 fusion.81
  22.2 1.3 copy-done.4
  23.5 3.3 broadcast_multiply_fusion.1
  27.5 1.3 eq.101
  28.8 2.1 reshape.287
  31.5 1.5 convolution_bitcast_fusion.2
  33.0 2.0 pad_maximum_fusion.1
  35.0 1.4 collective-permute-start.1
  36.4 5.3 convolution_bitcast_fusion.1
  41.8 28.4 %reshape.288 = f32[24,16,16,16,16]{4,3,2,1,0:T(8,128)} reshape(f32[24,256,256]{2,1,0:T(8,128)} %convolution_bitcast_fusion.1) | data formatting | bytes 12582912 | tf_op jit(solution)/shard_map/reshape | solution.py:108
  70.2 50.9 %copy.45 = f32[24,16,16,16,16]{2,1,4,3,0:T(8,128)} copy(f32[24,16,16,16,16]{4,2,3,1,0:T(8,128)} %bitcast.132) | data formatting | bytes 12582912 | tf_op jit(solution)/shard_map/reshape | solution.py:109
  121.0 34.6 %reshape.296 = f32[24,256,256]{1,2,0:T(8,128)} reshape(f32[24,16,16,16,16]{2,1,4,3,0:T(8,128)} %copy.45) | data formatting | bytes 12582912 | tf_op jit(solution)/shard_map/reshape | solution.py:109
  155.7 0.8 fusion.58
  156.5 1.1 pad_maximum_fusion.5
  157.6 0.7 copy-done.9
  158.3 2.5 convolution_bitcast_fusion
  160.9 3.6 copy.29
  164.5 1.6 multiply_reduce_fusion.5
  166.2 7.7 %fusion.2 = (f32[24,256]{1,0:T(8,128)S(1)}, f32[24,256,256]{1,2,0:T(8,128)}) fusion(f32[256,256]{0,1:T(8,128)} %fusion.58, f32[24,256,256]{1,2,0:T(8,128)} %reshape.296, f32[24,256]{1,0:T(8,128)S(1)} %get-tuple-element.101, f32[1,3,24,32,256]{4,3,2,1,0:T(8,128)} %bitcast.137, f32[24]{0:T(128)S(1)} %exp.13, f32[24,256]{1,0:T(8,128)S(1)} %get-tuple-element.100), kind=kOutput, calls=%fused_computation.13 | convolution fusion | flops 106358784 | bytes 14491744 | tf_op jit(solution)/shard_map/while/body/eval_jaxpr/hdi,hdj->hij/dot_general | solution.py:130
  173.9 4.1 broadcast_divide_fusion
  178.0 2.5 fusion.32
  182.1 1.1 multiply_reduce_fusion.4
  185.2 1.5 multiply_convert_fusion
  186.7 0.8 copy-done.17
  187.5 2.5 fusion.35
  190.0 1.9 copy.33
  192.0 4.8 fusion.17
  196.8 6.5 multiply_reduce_fusion.1
  203.3 10.0 %multiply_reduce_fusion = (f32[24]{0:T(128)S(1)}, f32[24,256,256]{1,2,0:T(8,128)}) fusion(f32[24,256,256]{1,2,0:T(8,128)} %get-tuple-element.78, f32[24,256,256]{1,2,0:T(8,128)} %copy-done.1, f32[24,256,256]{1,2,0:T(8,128)} %get-tuple-element.97, f32[24,256]{1,0:T(8,128)S(1)} %get-tuple-element.96), kind=kLoop, calls=%fused_computation.2 | loop fusion | flops 6291432 | bytes 25190496 | tf_op jit(solution)/shard_map/while/body/eval_jaxpr/reduce_sum | solution.py:186
  213.2 4.9 fusion.9
  218.1 1.6 fusion.20
  219.7 1.5 convolution_convert_fusion.1
  221.2 6.7 copy.38
  227.9 2.2 fusion.27
  230.2 1.7 fusion.30
  232.1 1.0 copy-done.12
  233.1 2.9 convolution_convert_fusion
  235.9 28.4 %reshape.293 = f32[24,16,16,16,16]{4,3,2,1,0:T(8,128)} reshape(f32[24,256,256]{2,1,0:T(8,128)} %copy.38) | data formatting | bytes 12582912 | tf_op jit(solution)/shard_map/while/body/eval_jaxpr/reshape | solution.py:164
  264.4 44.6 %copy.39 = f32[24,16,16,16,16]{4,3,2,1,0:T(8,128)} copy(f32[24,16,16,16,16]{4,2,3,1,0:T(8,128)} %bitcast.133) | data formatting | bytes 12582912 | tf_op jit(solution)/shard_map/while/body/eval_jaxpr/transpose | solution.py:164
  309.0 34.6 %dot_general.91 = f32[24,256,256]{2,1,0:T(8,128)} reshape(f32[24,16,16,16,16]{4,3,2,1,0:T(8,128)} %copy.39) | data formatting | bytes 12582912 | tf_op jit(solution)/shard_map/while/body/eval_jaxpr/dot_general | solution.py:165
  343.6 5.9 fusion.67
  349.5 1.8 convolution_bitcast_fusion.3
  351.4 5.1 pad_maximum_fusion
  356.5 2.5 fusion.31
  359.0 0.7 copy-done.19
  359.8 0.7 slice.55
  360.5 78.6 %all-reduce = (f32[768]{0:T(1024)}, f32[24]{0:T(128)}) all-reduce(f32[768]{0:T(1024)S(1)} %get-tuple-element.67, f32[24]{0:T(128)S(1)} %get-tuple-element.71), channel_id=1, replica_groups=mesh['lat'=8,'lon'=32] {'lat','lon'}, use_global_device_ids=true, to_apply=%region_13.14 | all-reduce | flops 792 | bytes 6336 | tf_op jit(solution)/shard_map/psum | solution.py:238
  439.1 158.6 %all-reduce.6.cloned.1.call-done = f32[31,31,24]{1,0,2:T(8,128)} async-done(((f32[31,31,24]{1,0,2:T(8,128)}), f32[31,31,24]{1,0,2:T(8,128)}) %all-reduce.6.cloned.1.call-update) | async-done | bytes 92272 | tf_op jit(solution)/shard_map/psum | solution.py:238
  597.6 1.8 broadcast_multiply_fusion
  599.4 1.8 mul.201
  601.3 5.6 fusion.80
  606.9 1.6 pad_maximum_fusion.10
  608.6 1.5 collective-permute-start.3
  610.0 2.0 fusion.3
  612.1 3.2 fusion.82
  615.3 2.5 collective-permute-done.3
  617.8 1.8 pad_maximum_fusion.3
  619.6 65.7 %all-reduce.4.cloned.1.call-done = bf16[24,3072]{1,0:T(8,128)(2,1)} async-done(((bf16[24,3072]{1,0:T(8,128)(2,1)}), bf16[24,3072]{1,0:T(8,128)(2,1)}) %all-reduce.4.cloned.1.call-update) | async-done | bytes 147472 | tf_op jit(solution)/shard_map/psum | solution.py:227
  685.3 1.6 slice.56
  686.9 1.4 slice.57
  (119 shorter events, 6.1 us)
Async XLA Ops:
  8.0 150.3 %copy-start = (bf16[768,2304]{1,0:T(8,128)(2,1)S(1)}, bf16[768,2304]{1,0:T(8,128)(2,1)}, u32[]{:S(2)}) copy-start(bf16[768,2304]{1,0:T(8,128)(2,1)} %param.12) | copy-start | bytes 10616836
  8.0 15.5 %copy-start.35 = (f32[512]{0:T(512)S(1)}, f32[512]{0:T(512)}, u32[]{:S(2)}) copy-start(f32[512]{0:T(512)} %param.17) | copy-start | bytes 6148
  8.0 589.6 %all-reduce.6.cloned.1.call-start = ((), (), s32[]{:S(2)}) async-start(), calls=%async_computation.3 | async-start | bytes 786432 | tf_op jit(solution)/shard_map/psum | solution.py:238
  10.0 23.0 %collective-permute-start = (bf16[2,16,8,768]{3,2,1,0:T(8,128)(2,1)}, bf16[2,16,8,768]{3,2,1,0:T(8,128)(2,1)}, u32[]{:S(2)}, u32[]{:S(2)}) collective-permute-start(bf16[2,16,8,768]{3,2,1,0:T(8,128)(2,1)} %pad_maximum_fusion.9), channel_id=1, source_target_pairs={{0,31},{1,0},{2,1},{3,2},{4,3},{5,4},{6,5},{7,6},{8,7},{9,8},{10,9... | collective-permute-start | bytes 1179656 | tf_op jit(solution)/shard_map/ppermute | solution.py:18
  19.7 15.3 %copy-start.31 = (f32[961,2]{0,1:T(2,128)}, f32[961,2]{0,1:T(2,128)S(1)}, u32[]{:S(2)}) copy-start(f32[961,2]{0,1:T(2,128)S(1)} %reshape.286) | copy-start | bytes 23068
  22.2 1.3 copy-start.4
  35.0 121.5 %collective-permute-start.1 = (bf16[2,8,24,768]{3,2,1,0:T(8,128)(2,1)}, bf16[2,8,24,768]{3,2,1,0:T(8,128)(2,1)}, u32[]{:S(2)}, u32[]{:S(2)}) collective-permute-start(bf16[2,8,24,768]{3,2,1,0:T(8,128)(2,1)} %pad_maximum_fusion.1), channel_id=1, source_target_pairs={{0,224},{32,0},{64,32},{96,64},{128,96},{160,128},{192,160},{224,1... | collective-permute-start | bytes 1769480 | tf_op jit(solution)/shard_map/ppermute | solution.py:18
  121.0 34.6 %copy-start.43 = (f32[24]{0:T(128)S(1)}, f32[24]{0:T(128)}, u32[]{:S(2)}) copy-start(f32[24]{0:T(128)} %param.15) | copy-start | bytes 292
  121.0 34.6 %copy-start.38 = (s32[256]{0:T(256)S(1)}, s32[256]{0:T(256)}, u32[]{:S(2)}) copy-start(s32[256]{0:T(256)} %eq.96) | copy-start | bytes 3076
  121.0 34.6 %copy-start.42 = (pred[256]{0:T(512)(128)(4,1)S(1)}, pred[256]{0:T(512)(128)(4,1)}, u32[]{:S(2)}) copy-start(pred[256]{0:T(512)(128)(4,1)} %eq.101) | copy-start | bytes 772
  155.7 10.5 %copy-start.40 = (f32[24]{0:T(128)}, f32[24]{0:T(128)S(1)}, u32[]{:S(2)}) copy-start(f32[24]{0:T(128)S(1)} %exp.13) | copy-start | bytes 292
  157.6 0.7 copy-start.9
  166.1 7.7 %copy-start.26 = (f32[24,256]{1,0:T(8,128)}, f32[24,256]{1,0:T(8,128)S(1)}, u32[]{:S(2)}) copy-start(f32[24,256]{1,0:T(8,128)S(1)} %get-tuple-element.100) | copy-start | bytes 73732
  166.1 7.7 %copy-start.29 = (f32[24,256]{1,0:T(8,128)}, f32[24,256]{1,0:T(8,128)S(1)}, u32[]{:S(2)}) copy-start(f32[24,256]{1,0:T(8,128)S(1)} %get-tuple-element.101) | copy-start | bytes 73732
  166.1 7.7 %slice-start = ((s8[6291456]{0:T(1024)(128)(4,1)}), s8[4194304]{0:T(1024)(128)(4,1)S(1)}, s32[]{:S(2)}) async-start(s8[6291456]{0:T(1024)(128)(4,1)} %bitcast.134), calls=%async_computation.4 | async-start | bytes 8388608
  166.1 7.7 %slice-start.1 = ((s8[6291456]{0:T(1024)(128)(4,1)}), s8[2097152]{0:T(1024)(128)(4,1)S(1)}, s32[]{:S(2)}) async-start(s8[6291456]{0:T(1024)(128)(4,1)} %bitcast.134), calls=%async_computation.5 | async-start | bytes 4194304
  166.1 7.7 %copy-start.21 = (f32[256,256]{0,1:T(8,128)S(1)}, f32[256,256]{0,1:T(8,128)}, u32[]{:S(2)}) copy-start(f32[256,256]{0,1:T(8,128)} %fusion.58) | copy-start | bytes 786436
  177.9 2.8 copy-start.1
  177.9 3.0 copy-start.11
  180.7 2.9 copy-start.14
  180.7 1.2 copy-start.7
  180.8 1.3 copy-start.8
  180.8 1.3 copy-start.33
  181.5 1.7 copy-start.6
  181.5 3.0 copy-start.37
  182.1 2.5 copy-start.39
  183.2 0.7 copy-start.16
  186.7 0.8 copy-start.17
  192.0 4.8 copy-start.3
  192.0 4.8 copy-start.13
  203.3 10.0 %copy-start.27 = (f32[24,256]{1,0:T(8,128)S(1)}, f32[24,256]{1,0:T(8,128)}, u32[]{:S(2)}) copy-start(f32[24,256]{1,0:T(8,128)} %copy-done.26) | copy-start | bytes 73732
  203.3 10.0 %copy-start.41 = (f32[24]{0:T(128)S(1)}, f32[24]{0:T(128)}, u32[]{:S(2)}) copy-start(f32[24]{0:T(128)} %copy-done.40) | copy-start | bytes 292
  213.2 4.9 copy-start.2
  213.2 4.9 copy-start.30
  218.1 1.6 copy-start.15
  218.1 1.6 copy-start.18
  227.9 2.2 copy-start.25
  227.9 2.2 copy-start.28
  230.1 1.7 copy-start.22
  230.2 2.9 copy-start.10
  232.0 1.0 copy-start.12
  309.0 34.6 %copy-start.34 = (s32[256]{0:T(256)S(1)}, s32[256]{0:T(256)}, u32[]{:S(2)}) copy-start(s32[256]{0:T(256)} %sub.112) | copy-start | bytes 3076
  351.3 260.7 %reduce-scatter.2.cloned.1.call-start = ((), (), s32[]{:S(2)}) async-start(), calls=%async_computation.1 | async-start | bytes 4866048 | tf_op jit(solution)/shard_map/reduce_scatter | solution.py:215
  356.5 328.9 %all-reduce.4.cloned.1.call-start = ((), (), s32[]{:S(2)}) async-start(), calls=%async_computation.2 | async-start | bytes 294912 | tf_op jit(solution)/shard_map/psum | solution.py:227
  356.5 244.7 %copy-start.36 = (f32[512]{0:T(512)S(1)}, f32[512]{0:T(512)}, u32[]{:S(2)}) copy-start(f32[512]{0:T(512)} %param.17) | copy-start | bytes 6148
  359.0 0.8 copy-start.19
  360.5 246.4 %collective-permute-start.2 = (bf16[16,8,768]{2,1,0:T(8,128)(2,1)}, bf16[16,8,768]{2,1,0:T(8,128)(2,1)}, u32[]{:S(2)}, u32[]{:S(2)}) collective-permute-start(bf16[16,8,768]{2,1,0:T(8,128)(2,1)} %slice.55), channel_id=1, source_target_pairs={{0,1},{1,2},{2,3},{3,4},{4,5},{5,6},{6,7},{7,8},{8,9},{9,10},{10,1... | collective-permute-start | bytes 589832 | tf_op jit(solution)/shard_map/ppermute | solution.py:18
  601.2 5.7 copy-start.20
  601.2 8.8 %copy-start.5 = (f32[961,512]{1,0:T(8,128)S(1)}, f32[961,512]{1,0:T(8,128)}, u32[]{:S(2)}) copy-start(f32[961,512]{1,0:T(8,128)} %copy-done.4) | copy-start | bytes 5904388
  601.2 8.8 %copy-start.23 = (f32[961,24]{0,1:T(8,128)S(1)}, f32[961,24]{0,1:T(8,128)}, u32[]{:S(2)}) copy-start(f32[961,24]{0,1:T(8,128)} %get-tuple-element.76) | copy-start | bytes 276772
  601.3 8.8 %copy-start.24 = (f32[961,24]{0,1:T(8,128)S(1)}, f32[961,24]{0,1:T(8,128)}, u32[]{:S(2)}) copy-start(f32[961,24]{0,1:T(8,128)} %mul.201) | copy-start | bytes 276772
  601.3 10.8 %copy-start.32 = (f32[961,2]{0,1:T(2,128)S(1)}, f32[961,2]{0,1:T(2,128)}, u32[]{:S(2)}) copy-start(f32[961,2]{0,1:T(2,128)} %copy-done.31) | copy-start | bytes 23068
  608.6 9.3 %collective-permute-start.3 = (bf16[8,24,768]{2,1,0:T(8,128)(2,1)}, bf16[8,24,768]{2,1,0:T(8,128)(2,1)}, u32[]{:S(2)}, u32[]{:S(2)}) collective-permute-start(bf16[8,24,768]{2,1,0:T(8,128)(2,1)} %pad_maximum_fusion.10), channel_id=1, source_target_pairs={{0,32},{32,64},{64,96},{96,128},{128,160},{160,192},{192,224},{224... | collective-permute-start | bytes 884744 | tf_op jit(solution)/shard_map/ppermute | solution.py:18
Sparse Core Ops, SparseCore 0:
  351.4 246.1 all-reduce.5
Sparse Core Ops, SparseCore 1:
  356.6 125.5 reduce-scatter.1
  612.2 73.1 all-reduce.3
where the time goes:
time: 710 us; the launch traced here: 696 us
  local copies, waits for them, and re-layouts  251 us (35%)
  waiting for transfers between devices  227 us (32%)
  blocking collectives  78.6 us (11%)
  matrix products  71.6 us (10%)
  other arithmetic  41.6 us (6%)
  between operations  16.2 us (2%)
  starting transfers between devices  9.89 us (1%)
    psum x1, waiting for transfers between devices, per_device(): lax.psum((gain_part, scale_sum, table_part), ('lat', 'lon'))  159 us
    reshape x2, local copies, waits for them, and re-layouts, per_device(): window_bias = jnp.transpose(window_bias.reshape(HEADS, WIN, WIN, WIN, WIN...  85.5 us
    psum x1, blocking collectives, per_device(): lax.psum((gain_part, scale_sum, table_part), ('lat', 'lon'))  78.6 us
    psum x1, waiting for transfers between devices, per_device(): both_total = lax.psum(both_part, 'lat').astype(jnp.float32)  65.7 us
    transpose x1, local copies, waits for them, and re-layouts, reduce_offsets(): jnp.transpose(dscores.reshape(HEADS, WIN, WIN, WIN, WIN), (0, 1, 3, 2, 4))  44.6 us
    dot_general x1, local copies, waits for them, and re-layouts, reduce_offsets(): jnp.dot(cube.reshape(HEADS * area, area), pair_table, precision=exact_mode)  34.6 us
    reshape x1, local copies, waits for them, and re-layouts, per_device(): window_bias.reshape(HEADS, WIN, WIN, WIN, WIN)  28.4 us
    reshape x1, local copies, waits for them, and re-layouts, reduce_offsets(): dscores.reshape(HEADS, WIN, WIN, WIN, WIN)  28.4 us
  transfers between devices with their start and end apart: 7, of which 3 were waited for; matrix products, arithmetic and copies ran while one was open for 23% of the time, Pallas kernels for 0%

commit v1 on v0

v1 whole, which is shorter than its diff:
```python
import functools

import jax
import jax.numpy as jnp
import numpy as np
from jax import lax
from jax.experimental import pallas as pl
from jax.experimental.pallas import tpu as pltpu
from jax.sharding import PartitionSpec as P

D = 768
HEADS = 24
HEAD_DIM = 32
HIDDEN = 512
WIN = 16
SHIFT = 8
AREA = WIN * WIN
QUAD = SHIFT * SHIFT
SLOTS = 1024
PART = 384
BLOCK = 24
BOTH = ("lat", "lon")
NEG = -1e30

f32 = jnp.float32
bf16 = jnp.bfloat16
exact = lax.Precision.HIGHEST

NN = (((1,), (0,)), ((), ()))
NT = (((1,), (1,)), ((), ()))
TN = (((0,), (0,)), ((), ()))


def mm(a, b, dims=NN, precision=None):
    return lax.dot_general(a, b, dims, precision=precision, preferred_element_type=f32)


def slot_coords():
    slot = lax.broadcasted_iota(jnp.int32, (SLOTS, 128), 0)
    row = (slot // 32) % 16 * 2 + slot // 512
    out = []
    for index in (row, slot % 32):
        spread = (index - (WIN - 1)).astype(f32) * (8.0 / (WIN - 1))
        size = jnp.log(1.0 + jnp.abs(spread)) * (1.0 / (3.0 * np.log(2.0)))
        out.append(jnp.concatenate([jnp.where(spread < 0.0, -size, size)] * 4, 1))
    return out


def hidden_of(inner_ref, offset_ref):
    first, second = slot_coords()
    before = first * inner_ref[0:1, :] + second * inner_ref[1:2, :] + offset_ref[...]
    return first, second, before, jnp.maximum(before, 0.0)


def fetch(pairs, sems, first=0):
    copies = [
        pltpu.make_async_copy(source, target, sems.at[first + n]) for n, (source, target) in enumerate(pairs)
    ]
    for copy in copies:
        copy.start()
    return copies


def cut_kernel(features_hbm, upstream_hbm, o00, o01, o10, o11, features_ref, upstream_ref, sems):
    outs = (o00, o01, o10, o11)
    for copy in fetch(((features_hbm, features_ref), (upstream_hbm, upstream_ref)), sems):
        copy.wait()
    feats = features_ref[...].astype(f32)
    ups = upstream_ref[...].astype(f32)
    for (r, c), out in zip(((8, 8), (8, 0), (0, 8), (0, 0)), outs):
        out[0:QUAD, :] = feats[r : r + 8, c : c + 8].reshape(QUAD, D).astype(bf16)
        out[QUAD:, :] = ups[r : r + 8, c : c + 8].reshape(QUAD, D).astype(bf16)


def bias_kernel(
    last_ref, log_ref, inner_hbm, offset_hbm, outer_hbm, valid_hbm,
    table_ref, mask_ref, factor_ref,
    inner_ref, offset_ref, outer_ref, valid_ref, rows_ref, in_sems,
):
    for copy in fetch(
        (
            (inner_hbm, inner_ref),
            (offset_hbm, offset_ref),
            (outer_hbm, outer_ref),
            (valid_hbm, valid_ref),
        ),
        in_sems,
    ):
        copy.wait()
    hidden = hidden_of(inner_ref, offset_ref)[3]
    logits = mm(outer_ref[...], hidden, NT, exact)
    grid = 16.0 * jax.nn.sigmoid(logits)
    even = grid[:, :512]
    odd = grid[:, 512:]
    lane = lax.broadcasted_iota(jnp.int32, (HEADS, 512), 1)
    first = (lane % 32) < 16
    for cj in range(WIN):
        rows_ref[cj] = jnp.where(
            first,
            pltpu.roll(even, (512 - 15 + cj) % 512, 1),
            pltpu.roll(odd, (1 + cj) % 512, 1),
        )
    valid = valid_ref[...].astype(f32).T
    split = last_ref[0] == 1
    cj = lax.broadcasted_iota(jnp.int32, (WIN, AREA), 0)
    query = lax.broadcasted_iota(jnp.int32, (WIN, AREA), 1)
    for rj in range(WIN):
        same = jnp.logical_or((query >= AREA // 2) == (rj >= WIN // 2), jnp.logical_not(split))
        seen = jnp.logical_or(valid[:, rj : rj + 1] == 1.0, rj * WIN + cj == query)
        mask_ref[rj * WIN : (rj + 1) * WIN, :] = jnp.where(jnp.logical_and(same, seen), 0.0, NEG)

    for head in range(HEADS):
        factor_ref[head] = jnp.exp(jnp.full((1, AREA), log_ref[head], f32))
        table_ref[head] = rows_ref[:, head : head + 1, :].reshape(WIN, 512)


def window_kernel(
    core_ref, factor_ref, table_ref, mask_ref, q00, q01, q10, q11, gain_hbm, weight_hbm, out_weight_hbm,
    send_ref, keep_ref, d00, d01, d10, d11, gain_out, scale_out, table_out,
    grid3, up, tokt, projt, exps, inv, hot, doutt, weight_ref, out_weight_ref, gain_ref, sems,
):
    weight_copies = [
        pltpu.make_async_copy(
            weight_hbm.at[:, part * PART : (part + 1) * PART],
            weight_ref.at[:, part * PART : (part + 1) * PART],
            sems.at[part],
        )
        for part in range(6)
    ]
    out_weight_copy = pltpu.make_async_copy(out_weight_hbm, out_weight_ref, sems.at[6])
    gain_copy = pltpu.make_async_copy(gain_hbm, gain_ref, sems.at[7])
    for copy in weight_copies:
        copy.start()
    gain_copy.start()
    out_weight_copy.start()

    places = ((0, 0), (0, 8), (8, 0), (8, 8))
    quads = (q00, q01, q10, q11)

    def assemble(rows):
        for (r, c), part in zip(places, quads):
            grid3[r : r + 8, c : c + 8, :] = part[rows, :].astype(f32).reshape(8, 8, D)
        return grid3[...].reshape(AREA, D)

    def rows_of(source, core):
        pieces = []
        for hi in range(2):
            for z in range(8):
                at = pl.multiple_of((hi * 16 + z * 2 + core) * BLOCK, 8)
                pieces.append(source[pl.ds(at, BLOCK), :])
        return jnp.concatenate(pieces, 0).astype(bf16)

    mine = core_ref[0]
    up[...] = assemble(slice(QUAD, 2 * QUAD))
    tokens32 = assemble(slice(0, QUAD))
    tokens = tokens32.astype(bf16)
    tokt[...] = tokens32.T
    for part in range(6):
        cols = slice(part * PART, (part + 1) * PART)
        weight_copies[part].wait()
        projt[cols, :] = mm(tokens, weight_ref[:, cols]).T
    keep_ref[0:384, :] = rows_of(tokt, mine)
    send_ref[0:384, :] = rows_of(tokt, 1 - mine)

    def head_inputs(head):
        at = pl.multiple_of(head * HEAD_DIM, HEAD_DIM)
        q = projt[pl.ds(at, HEAD_DIM), :]
        k = projt[pl.ds(D + at, HEAD_DIM), :]
        v = projt[pl.ds(2 * D + at, HEAD_DIM), :]
        q_inv = lax.rsqrt(jnp.sum(q * q, 0, keepdims=True) + 1.0)
        k_inv = lax.rsqrt(jnp.sum(k * k, 0, keepdims=True) + 1.0)
        q_unit = q * q_inv
        k_unit = k * k_inv
        factor = factor_ref[head]
        return at, q_unit, q_inv, (q_unit * factor).astype(bf16), k_unit, k_inv, k_unit.astype(bf16), v, factor

    extra = lax.broadcasted_iota(jnp.int32, (16, AREA), 0)

    def forward_head(head, carry):
        at, _, _, q_round, _, _, k_round, v, _ = head_inputs(head)
        scores = mm(k_round, q_round, TN)
        table = table_ref[head]
        slabs = [None] * WIN
        for b in range(8):
            turned = table if b == 0 else pltpu.roll(table, 512 - 16 * b, 1)
            for a in range(2):
                rj = 15 - (8 * a + b)
                rows = slice(rj * 16, rj * 16 + 16)
                slabs[rj] = jnp.exp(
                    scores[rows, :] + (turned[:, 128 * a : 128 * a + 256] + mask_ref[rows, :])
                ).astype(bf16)
        weights = jnp.concatenate(slabs, 0)
        exps[head] = weights
        values = jnp.concatenate([v, jnp.where(extra == 0, 1.0, 0.0)], 0).astype(bf16)
        mixed = mm(values, weights)
        inverse = 1.0 / mixed[HEAD_DIM : HEAD_DIM + 1, :]
        inv[head] = inverse
        hot[pl.ds(at, HEAD_DIM), :] = mixed[:HEAD_DIM, :] * inverse
        return carry

    lax.fori_loop(0, HEADS, forward_head, 0, unroll=12)

    keep_ref[384:768, :] = rows_of(hot, mine)
    send_ref[384:768, :] = rows_of(hot, 1 - mine)
    out_weight_copy.wait()
    gain_copy.wait()
    heads_out = hot[...].T.astype(bf16)
    mixed_out = mm(heads_out, out_weight_ref[...])
    centre = jnp.mean(mixed_out, -1, keepdims=True)
    shifted = mixed_out - centre
    inverse = lax.rsqrt(jnp.mean(shifted * shifted, -1, keepdims=True) + 1e-05)
    normed = shifted * inverse
    up_now = up[...]
    gain_out[...] = jnp.sum(up_now * normed, 0, keepdims=True)
    dnormed = up_now * gain_ref[...].reshape(1, D)
    dmixed = (
        dnormed
        - jnp.mean(dnormed, -1, keepdims=True)
        - normed * jnp.mean(dnormed * normed, -1, keepdims=True)
    ) * inverse
    dmixed = dmixed.astype(bf16)
    for part in range(3):
        send_ref[3072 + part * AREA : 3072 + (part + 1) * AREA, :] = dmixed[:, part * AREA : (part + 1) * AREA]
    doutt[...] = mm(out_weight_ref[...], dmixed, NT).astype(bf16)

    def backward_head(head, carry):
        at, q_unit, q_inv, q_round, k_unit, k_inv, k_round, v, factor = head_inputs(head)
        weights = exps[head]
        inverse = inv[head]
        dout = (doutt[pl.ds(at, HEAD_DIM), :].astype(f32) * inverse).astype(bf16).astype(f32)
        delta = jnp.sum(dout * hot[pl.ds(at, HEAD_DIM), :], 0, keepdims=True)
        high = delta.astype(bf16).astype(f32)
        tail = jnp.where(extra == 0, high, jnp.where(extra == 1, delta - high, 0.0))
        dout_more = jnp.concatenate([dout, tail], 0).astype(bf16)
        values = jnp.concatenate([v, jnp.where(extra < 2, -1.0, 0.0)], 0).astype(bf16)
        dscores = weights.astype(f32) * mm(values, dout_more, TN)
        dround = dscores.astype(bf16)
        dvalue = mm(dout.astype(bf16), weights, NT)
        dquery = mm(k_round, dround)
        dkey = mm(q_round, dround, NT)
        scale_out[pl.ds(head, 1), :] = jnp.sum(dscores * mm(k_round, q_round, TN), 0, keepdims=True)
        dquery = dquery * factor
        dquery = (dquery - q_unit * jnp.sum(q_unit * dquery, 0, keepdims=True)) * q_inv
        dkey = (dkey - k_unit * jnp.sum(k_unit * dkey, 0, keepdims=True)) * k_inv
        send_ref[pl.ds(768 + at, HEAD_DIM), :] = dquery.astype(bf16)
        send_ref[pl.ds(768 + D + at, HEAD_DIM), :] = dkey.astype(bf16)
        send_ref[pl.ds(768 + 2 * D + at, HEAD_DIM), :] = dvalue.astype(bf16)
        total = None
        for b in range(8):
            near = dscores[(15 - b) * 16 : (15 - b) * 16 + 16, :]
            far = dscores[(7 - b) * 16 : (7 - b) * 16 + 16, :]
            wide = jnp.concatenate(
                [near[:, :128], near[:, 128:] + far[:, :128], far[:, 128:], jnp.zeros((16, 128), f32)], 1
            )
            if b:
                wide = pltpu.roll(wide, 16 * b, 1)
            total = wide if total is None else total + wide
        table_out[head] = total
        return carry

    lax.fori_loop(0, HEADS, backward_head, 0, unroll=24)

    dtokens = up[...] + mm(weight_ref[...], send_ref[768:3072, :]).T
    grid3[...] = dtokens.reshape(WIN, WIN, D)
    for (r, c), part in zip(places, (d00, d01, d10, d11)):
        part[...] = grid3[r : r + 8, c : c + 8, :].reshape(QUAD, D).astype(bf16)


def table_kernel(
    inner_hbm, offset_hbm, outer_hbm, table_ref, gain_ref, scale_ref,
    pack_ref,
    inner_ref, offset_ref, outer_ref, rows_ref, work_ref, sems,
):
    for copy in fetch(((inner_hbm, inner_ref), (offset_hbm, offset_ref), (outer_hbm, outer_ref)), sems):
        copy.wait()
    first_coord, second_coord, before, hidden = hidden_of(inner_ref, offset_ref)
    logits = mm(outer_ref[...], hidden, NT, exact)
    sig = jax.nn.sigmoid(logits)
    lane = lax.broadcasted_iota(jnp.int32, (HEADS, 512), 1)
    first = (lane % 32) < 16
    for head in range(HEADS):
        rows_ref[:, head : head + 1, :] = table_ref[head].reshape(WIN, 1, 512)
    even = jnp.zeros((HEADS, 512), f32)
    odd = jnp.zeros((HEADS, 512), f32)
    for cj in range(WIN):
        row = rows_ref[cj]
        even = even + pltpu.roll(jnp.where(first, row, 0.0), 15 - cj, 1)
        odd = odd + pltpu.roll(jnp.where(first, 0.0, row), (512 - 1 - cj) % 512, 1)
    dgrid = jnp.concatenate([even, odd], 1)
    dlogits = 16.0 * dgrid * sig * (1.0 - sig)
    outer = mm(dlogits, hidden, NN, exact)
    dhidden = mm(dlogits, outer_ref[...], TN, exact)
    dhidden = jnp.where(before > 0.0, dhidden, 0.0)
    scale = jnp.sum(scale_ref[...], -1, keepdims=True)
    where_row = lax.broadcasted_iota(jnp.int32, (HEADS, PART), 0)
    where_lane = lax.broadcasted_iota(jnp.int32, (HEADS, PART), 1)
    first_inner = jnp.sum(first_coord * dhidden, 0, keepdims=True)
    second_inner = jnp.sum(second_coord * dhidden, 0, keepdims=True)
    offset = jnp.sum(dhidden, 0, keepdims=True)
    work_ref[0:HEADS, :] = outer[:, :PART]
    for head in range(HEADS):
        place = (head % 3) * 128
        work_ref[24 + head // 3 : 25 + head // 3, place : place + 128] = outer[head : head + 1, PART:]
    work_ref[32:33, :] = first_inner[:, :PART]
    work_ref[33:34, :] = second_inner[:, :PART]
    work_ref[34:35, :] = jnp.concatenate([first_inner[:, PART:], second_inner[:, PART:], offset[:, PART:]], 1)
    work_ref[35:36, :] = offset[:, :PART]
    work_ref[36:37, :] = gain_ref[:, :PART]
    work_ref[37:38, :] = gain_ref[:, PART:]
    work_ref[38:39, :] = jnp.sum(jnp.where(where_row == where_lane, scale, 0.0), 0, keepdims=True)
    work_ref[39:64, :] = jnp.zeros((25, PART), f32)
    pack_ref[...] = work_ref[...].astype(bf16)


def grads_kernel(keep_ref, send_ref, got_ref, pack_ref, got_pack_ref, out_ref):
    pack = pack_ref[...].astype(f32) + got_pack_ref[...].astype(f32)
    for part in range(8):
        for hi in range(2):
            total = None
            for own, source in ((keep_ref, send_ref), (got_ref, got_ref)):
                base = hi * 192 + (384 if part >= 6 else 0)
                rows = own[base : base + 192, :]
                if part < 6:
                    piece = mm(rows, source[768 + part * PART : 768 + (part + 1) * PART, :], NT)
                else:
                    first = 3072 if part == 6 else 3072 + AREA
                    halves = [
                        mm(rows, source[first + n * AREA : first + (n + 1) * AREA, :]) for n in range(2)
                    ]
                    if part == 6:
                        piece = jnp.concatenate([halves[0], halves[1][:, :128]], 1)
                    else:
                        piece = jnp.concatenate([halves[0][:, 128:], halves[1]], 1)
                total = piece if total is None else total + piece
            out_ref[hi * 8 + part] = jnp.concatenate([total, pack[part * 8 : part * 8 + 8]], 0).astype(bf16)


def plane_kernel(in_ref, out_ref):
    total = in_ref[0].astype(f32)
    for n in range(1, 16):
        total = total + in_ref[n].astype(f32)
    for z in range(8):
        out_ref[z] = jnp.concatenate([total[z * BLOCK : (z + 1) * BLOCK], total[192:200]], 0).astype(bf16)


def column_kernel(in_ref, out_ref):
    total = in_ref[0].astype(f32)
    for n in range(1, 8):
        total = total + in_ref[n].astype(f32)
    both = total.astype(bf16)
    for n in range(8):
        out_ref[n] = both


def finish_kernel(in_ref, attend_ref, output_ref, gain_ref, scale_ref, inner_ref, offset_ref, outer_ref, work_ref):
    for part in range(8):
        piece = in_ref[part].astype(f32)
        if part < 6:
            attend_ref[:, part * PART : (part + 1) * PART] = piece[:BLOCK]
        else:
            output_ref[:, (part - 6) * PART : (part - 5) * PART] = piece[:BLOCK]
        work_ref[part * 8 : part * 8 + 8, :] = piece[24:32]
    tails = [
        work_ref[24 + head // 3 : 25 + head // 3, (head % 3) * 128 : (head % 3) * 128 + 128] for head in range(HEADS)
    ]
    outer = jnp.concatenate([work_ref[0:HEADS, :], jnp.concatenate(tails, 0)], 1)
    outer_ref[...] = outer
    inner_ref[0:1, :PART] = work_ref[32:33, :]
    inner_ref[1:2, :PART] = work_ref[33:34, :]
    inner_ref[0:1, PART:] = work_ref[34:35, 0:128]
    inner_ref[1:2, PART:] = work_ref[34:35, 128:256]
    offset_ref[...] = jnp.concatenate([work_ref[35:36, :], work_ref[34:35, 256:]], 1).reshape(HIDDEN)
    gain_ref[...] = jnp.concatenate([work_ref[36:37, :], work_ref[37:38, :]], 1).reshape(D)
    scale_ref[...] = work_ref[38:39, :].reshape(PART)[:HEADS]


def vmem(count):
    return [pl.BlockSpec(memory_space=pltpu.VMEM)] * count


HBM = pl.BlockSpec(memory_space=pltpu.MemorySpace.HBM)
SMEM = pl.BlockSpec(memory_space=pltpu.SMEM)


def params(mib):
    return pltpu.CompilerParams(vmem_limit_bytes=mib * 1024 * 1024)


def cost(micros):
    return pl.CostEstimate(flops=int(micros * 1.15e9), bytes_accessed=0, transcendentals=0)


def place_of(lat, hi, z, core):
    return lat * 32 + hi * 16 + z * 2 + core


def shift_pairs(lat_step, lon_step):
    return [
        (lat * 32 + lon, ((lat + lat_step) % 8) * 32 + (lon + lon_step) % 32)
        for lat in range(8)
        for lon in range(32)
    ]


PLANE = [[place_of(lat, hi, z, core) for hi in range(2) for lat in range(8)] for z in range(8) for core in range(2)]
COLUMN = [[place_of(lat, hi, z, core) for z in range(8)] for lat in range(8) for hi in range(2) for core in range(2)]
LATS = [[place_of(lat, hi, z, core) for lat in range(8)] for hi in range(2) for z in range(8) for core in range(2)]
CORES = [
    (place_of(lat, hi, z, core), place_of(lat, hi, z, 1 - core))
    for lat in range(8)
    for hi in range(2)
    for z in range(8)
    for core in range(2)
]


def exchange(value, groups):
    return lax.all_to_all(value, BOTH, 0, 0, axis_index_groups=groups, tiled=True)


def per_device(
    features, upstream, attend_weight, output_weight, norm_gain, logit_scale,
    table_inner, table_offset, table_outer, validity,
):
    steps = ((0, 0), (0, 1), (1, 0), (1, 1))
    both = pl.pallas_call(
        cut_kernel,
        out_shape=(jax.ShapeDtypeStruct((2 * QUAD, D), bf16),) * 4,
        in_specs=[HBM] * 2,
        out_specs=tuple(vmem(4)),
        scratch_shapes=[pltpu.VMEM((WIN, WIN, D), bf16)] * 2 + [pltpu.SemaphoreType.DMA((2,))],
        compiler_params=params(16),
        cost_estimate=cost(2),
        name="cut",
    )(features, upstream)
    moved = [
        value if step == (0, 0) else lax.ppermute(value, BOTH, shift_pairs(-step[0], -step[1]))
        for step, value in zip(steps, both)
    ]

    outer_t = table_outer.T
    offset_row = table_offset.reshape(1, HIDDEN)
    last = (lax.axis_index("lat") == lax.axis_size("lat") - 1).astype(jnp.int32).reshape(1)
    core = (lax.axis_index("lon") % 2).astype(jnp.int32).reshape(1)
    bias, mask, factor = pl.pallas_call(
        bias_kernel,
        out_shape=(
            jax.ShapeDtypeStruct((HEADS, WIN, 512), f32),
            jax.ShapeDtypeStruct((AREA, AREA), f32),
            jax.ShapeDtypeStruct((HEADS, 1, AREA), f32),
        ),
        in_specs=[SMEM] * 2 + [HBM] * 4,
        out_specs=tuple(vmem(3)),
        scratch_shapes=[
            pltpu.VMEM((2, HIDDEN), f32),
            pltpu.VMEM((1, HIDDEN), f32),
            pltpu.VMEM((HEADS, HIDDEN), f32),
            pltpu.VMEM((WIN, WIN), jnp.int32),
            pltpu.VMEM((WIN, HEADS, 512), f32),
            pltpu.SemaphoreType.DMA((4,)),
        ],
        compiler_params=params(16),
        cost_estimate=cost(30),
        name="bias",
    )(last, logit_scale, table_inner, offset_row, outer_t, validity)

    quad_shape = jax.ShapeDtypeStruct((QUAD, D), bf16)
    send, keep, *dquads, gain_part, scale_part, table_part = pl.pallas_call(
        window_kernel,
        out_shape=(
            jax.ShapeDtypeStruct((3840, AREA), bf16),
            jax.ShapeDtypeStruct((768, AREA), bf16),
            quad_shape,
            quad_shape,
            quad_shape,
            quad_shape,
            jax.ShapeDtypeStruct((1, D), f32),
            jax.ShapeDtypeStruct((HEADS, AREA), f32),
            jax.ShapeDtypeStruct((HEADS, WIN, 512), f32),
        ),
        in_specs=[SMEM] + vmem(7) + [HBM] * 3,
        out_specs=tuple(vmem(9)),
        scratch_shapes=[
            pltpu.VMEM((WIN, WIN, D), f32),
            pltpu.VMEM((AREA, D), f32),
            pltpu.VMEM((D, AREA), f32),
            pltpu.VMEM((3 * D, AREA), f32),
            pltpu.VMEM((HEADS, AREA, AREA), bf16),
            pltpu.VMEM((HEADS, 1, AREA), f32),
            pltpu.VMEM((D, AREA), f32),
            pltpu.VMEM((D, AREA), bf16),
            pltpu.VMEM((D, 3 * D), bf16),
            pltpu.VMEM((D, D), bf16),
            pltpu.VMEM((D,), f32),
            pltpu.SemaphoreType.DMA((8,)),
        ],
        compiler_params=params(36),
        cost_estimate=cost(17),
        name="window",
    )(core, factor, bias, mask, *moved, norm_gain, attend_weight, output_weight)

    got = lax.ppermute(send, BOTH, CORES)
    pack = pl.pallas_call(
        table_kernel,
        out_shape=jax.ShapeDtypeStruct((64, PART), bf16),
        in_specs=[HBM] * 3 + vmem(3),
        out_specs=vmem(1)[0],
        scratch_shapes=[
            pltpu.VMEM((2, HIDDEN), f32),
            pltpu.VMEM((1, HIDDEN), f32),
            pltpu.VMEM((HEADS, HIDDEN), f32),
            pltpu.VMEM((WIN, HEADS, 512), f32),
            pltpu.VMEM((64, PART), f32),
            pltpu.SemaphoreType.DMA((3,)),
        ],
        compiler_params=params(16),
        cost_estimate=cost(5),
        name="table",
    )(table_inner, offset_row, outer_t, table_part, gain_part, scale_part)
    got_pack = lax.ppermute(pack, BOTH, CORES)
    grads = pl.pallas_call(
        grads_kernel,
        out_shape=jax.ShapeDtypeStruct((16, 200, PART), bf16),
        in_specs=vmem(5),
        out_specs=vmem(1)[0],
        compiler_params=params(24),
        cost_estimate=cost(2),
        name="grads",
    )(keep, send, got, pack, got_pack)
    plane = pl.pallas_call(
        plane_kernel,
        out_shape=jax.ShapeDtypeStruct((8, 32, PART), bf16),
        in_specs=vmem(1),
        out_specs=vmem(1)[0],
        compiler_params=params(16),
        cost_estimate=cost(1),
        name="plane",
    )(exchange(grads, PLANE))
    late = lax.optimization_barrier((plane, *dquads))
    plane, dquads = late[0], late[1:]
    back = [
        value if step == (0, 0) else lax.ppermute(value, BOTH, shift_pairs(*step))
        for step, value in zip(steps, dquads)
    ]
    held = lax.optimization_barrier((exchange(plane, COLUMN), *back))
    column, back = held[0], held[1:]
    column = pl.pallas_call(
        column_kernel,
        out_shape=jax.ShapeDtypeStruct((8, 32, PART), bf16),
        in_specs=vmem(1),
        out_specs=vmem(1)[0],
        compiler_params=params(16),
        cost_estimate=cost(1),
        name="column",
    )(column)

    back = [value.reshape(SHIFT, SHIFT, D) for value in back]
    input_delta = jnp.concatenate(
        [jnp.concatenate([back[3], back[2]], 1), jnp.concatenate([back[1], back[0]], 1)], 0
    )

    attend_delta, output_delta, gain, scale, inner, offset, outer = pl.pallas_call(
        finish_kernel,
        out_shape=(
            jax.ShapeDtypeStruct((BLOCK, 3 * D), f32),
            jax.ShapeDtypeStruct((BLOCK, D), f32),
            jax.ShapeDtypeStruct((D,), f32),
            jax.ShapeDtypeStruct((HEADS,), f32),
            jax.ShapeDtypeStruct((2, HIDDEN), f32),
            jax.ShapeDtypeStruct((HIDDEN,), f32),
            jax.ShapeDtypeStruct((HEADS, HIDDEN), f32),
        ),
        in_specs=vmem(1),
        out_specs=tuple(vmem(7)),
        scratch_shapes=[pltpu.VMEM((64, PART), f32)],
        compiler_params=params(16),
        cost_estimate=cost(1),
        name="finish",
    )(exchange(column, LATS))
    return (
        input_delta,
        attend_delta,
        output_delta,
        gain,
        scale,
        inner,
        offset,
        outer.T,
    )


def solution(mesh):
    in_specs = (
        P("lat", "lon", None),
        P("lat", "lon", None),
        P(),
        P(),
        P(),
        P(),
        P(),
        P(),
        P(),
        P("lat", "lon"),
    )
    out_specs = (P("lat", "lon", None), P("lon", None), P("lon", None), P(), P(), P(), P(), P())
    return jax.shard_map(
        per_device, mesh=mesh, in_specs=in_specs, out_specs=out_specs, check_vma=False
    )
```

time: 710 us -> 118 us (0.17); the launches traced: 696 us -> 117 us
  local copies, waits for them, and re-layouts: 251 us -> 5.66 us
  waiting for transfers between devices: 227 us -> 15.6 us
  matrix products: 71.6 us -> 0 us
  other arithmetic: 41.6 us -> 0.77 us
  blocking collectives: 78.6 us -> 38.3 us
  Pallas kernels: 0 us -> 31.4 us
  between operations: 16.2 us -> 0.76 us
  starting transfers between devices: 9.89 us -> 24.7 us
    psum x2 -> x0, waiting for transfers between devices: 224 us -> none  [the longest x1 159 us: per_device(): lax.psum((gain_part, scale_sum, table_part), ('lat', 'lon'))]
    reshape x6 -> x0, local copies, waits for them, and re-layouts: 145 us -> none  [the longest x2 85.5 us: per_device(): window_bias = jnp.transpose(window_bias.reshape(HEADS, WIN, WIN, WIN, WIN...]
    psum x1 -> x0, blocking collectives: 78.6 us -> none  [per_device(): lax.psum((gain_part, scale_sum, table_part), ('lat', 'lon'))]
    dot_general x21 -> x0, matrix products: 71.6 us -> none  [the longest x1 7.68 us: attention_weights(): jnp.einsum('hdi,hdj->hij', query_block, key_block, preferred_element_type...]
    transpose x3 -> x0, local copies, waits for them, and re-layouts: 50.1 us -> none  [the longest x1 44.6 us: reduce_offsets(): jnp.transpose(dscores.reshape(HEADS, WIN, WIN, WIN, WIN), (0, 1, 3, 2, 4))]
    all_to_all x0 -> x1, blocking collectives: none -> 38.3 us  [exchange(): lax.all_to_all(value, BOTH, 0, 0, axis_index_groups=groups, tiled=True)]
    dot_general x1 -> x0, local copies, waits for them, and re-layouts: 34.6 us -> none  [reduce_offsets(): jnp.dot(cube.reshape(HEADS * area, area), pair_table, precision=exact_mode)]
    pallas_call x0 -> x8, Pallas kernels: none -> 31.4 us  [the longest x1 17.5 us: per_device(): pl.pallas_call(window_kernel, out_shape=(jax.ShapeDtypeStruct((3840, AREA...]
  transfers between devices with their start and end apart: 7 -> 10, of which waited for: 3 -> 7; matrix products, arithmetic and copies ran while one was open for 23% -> 1% of each run, Pallas kernels for 0% -> 8%
where the time goes in v1:
time: 118 us; the launch traced here: 117 us
  blocking collectives  38.3 us (32%)
  Pallas kernels  31.4 us (27%)
  starting transfers between devices  24.7 us (21%)
  waiting for transfers between devices  15.6 us (13%)
  local copies, waits for them, and re-layouts  5.66 us (5%)
    all_to_all x1, blocking collectives, exchange(): lax.all_to_all(value, BOTH, 0, 0, axis_index_groups=groups, tiled=True)  38.3 us
    pallas_call x1, Pallas kernels, per_device(): pl.pallas_call(window_kernel, out_shape=(jax.ShapeDtypeStruct((3840, AREA...  17.5 us
    all_to_all x2, starting transfers between devices, exchange(): lax.all_to_all(value, BOTH, 0, 0, axis_index_groups=groups, tiled=True)  11.2 us
    ppermute x3, starting transfers between devices, per_device(): lax.ppermute(value, BOTH, shift_pairs(-step[0], -step[1]))  10.3 us
    ppermute x3, waiting for transfers between devices, per_device(): lax.ppermute(value, BOTH, shift_pairs(*step))  7.15 us
    all_to_all x2, waiting for transfers between devices, exchange(): lax.all_to_all(value, BOTH, 0, 0, axis_index_groups=groups, tiled=True)  6.52 us
    unnamed x24, local copies, waits for them, and re-layouts  5.66 us
    pallas_call x1, Pallas kernels, per_device(): pl.pallas_call(table_kernel, out_shape=jax.ShapeDtypeStruct((64, PART), b...  5.43 us
  transfers between devices with their start and end apart: 10, of which 7 were waited for; matrix products, arithmetic and copies ran while one was open for 1% of the time, Pallas kernels for 8%

profile of v1, /device:TPU:2, one launch (start us, length us, event | category | flops | bytes accessed | tf_op | source)
XLA Modules:
  0.0 117.2 jit_solution(6540234499339638394)
XLA Ops:
  0.6 0.0 copy-start.2
  0.6 1.0 copy-done.2
  1.6 0.0 copy-start.3
  1.6 1.0 copy-done.3
  2.6 0.0 copy-start.4
  2.6 0.0 copy-start.5
  2.6 0.0 copy-start.7
  2.6 0.0 copy-start.8
  2.6 0.0 copy-start.9
  2.6 0.4 cut.1
  3.1 6.9 %collective-permute-start = (bf16[128,768]{1,0:T(8,128)(2,1)S(1)}, bf16[128,768]{1,0:T(8,128)(2,1)S(1)}, u32[]{:S(2)}, u32[]{:S(2)}) collective-permute-start(bf16[128,768]{1,0:T(8,128)(2,1)S(1)} %get-tuple-element.45), channel_id=1, source_target_pairs={{0,31},{1,0},{2,1},{3,2},{4,3},{5,4},{6,5},{7,6},{8,7},{9,8},{10,9... | collective-permute-start | bytes 589832 | tf_op jit(solution)/shard_map/ppermute | solution.py:437
  10.0 1.4 %collective-permute-start.1 = (bf16[128,768]{1,0:T(8,128)(2,1)S(1)}, bf16[128,768]{1,0:T(8,128)(2,1)S(1)}, u32[]{:S(2)}, u32[]{:S(2)}) collective-permute-start(bf16[128,768]{1,0:T(8,128)(2,1)S(1)} %get-tuple-element.46), channel_id=1, source_target_pairs={{0,224},{1,225},{2,226},{3,227},{4,228},{5,229},{6,230},{7,231},{8... | collective-permute-start | bytes 589832 | tf_op jit(solution)/shard_map/ppermute | solution.py:437
  11.5 2.0 %collective-permute-start.2 = (bf16[128,768]{1,0:T(8,128)(2,1)S(1)}, bf16[128,768]{1,0:T(8,128)(2,1)S(1)}, u32[]{:S(2)}, u32[]{:S(2)}) collective-permute-start(bf16[128,768]{1,0:T(8,128)(2,1)S(1)} %get-tuple-element.47), channel_id=1, source_target_pairs={{0,255},{1,224},{2,225},{3,226},{4,227},{5,228},{6,229},{7,230},{8... | collective-permute-start | bytes 589832 | tf_op jit(solution)/shard_map/ppermute | solution.py:437
  13.4 0.0 copy-done.4
  13.5 0.0 copy-done.5
  13.5 0.0 copy-done.7
  13.5 0.0 copy-done.8
  13.5 0.0 copy-done.9
  13.5 0.0 copy-start.1
  13.5 0.0 copy-start.6
  13.5 3.5 %bias.1 = (f32[24,16,512]{2,1,0:T(8,128)S(1)}, f32[256,256]{1,0:T(8,128)S(1)}, f32[24,1,256]{2,1,0:T(1,128)S(1)}) custom-call(s32[1]{0:T(128)} %bitcast.1.last_ref, f32[24]{0:T(128)S(1)} %copy-done.9, f32[2,512]{1,0:T(2,128)S(1)} %copy-done.7, f32[1,512]{1,0:T(1,128)S(1)} %bitcast.12, f32[24,512]{1,0:T(8,128)S(1)} %bitcast.10, s32[16,16]{1,0:T(8,128)S(1)} %copy-done.5), custom_call_target="tpu_custom_call" | custom-call | flops 34500001792 | tf_op jit(solution)/shard_map/bias/pallas_call | solution.py:445
  17.0 0.0 copy-start.10
  17.0 0.7 copy-done.10
  17.7 0.0 collective-permute-done.q01
  17.7 0.2 collective-permute-done.1.q10
  17.9 0.8 collective-permute-done.2.q11
  18.7 0.0 copy-done.1
  18.7 0.0 copy-done.6
  18.7 0.0 copy-start
  18.7 2.0 %copy-done = bf16[768,2304]{1,0:T(8,128)(2,1)S(1)} copy-done((bf16[768,2304]{1,0:T(8,128)(2,1)S(1)}, bf16[768,2304]{1,0:T(8,128)(2,1)}, u32[]{:S(2)}) %copy-start) | copy-done | bytes 3538968
  20.7 0.0 copy-start.11
  20.7 0.9 copy-done.11
  21.7 17.5 %window.1 = (bf16[3840,256]{1,0:T(8,128)(2,1)S(1)}, bf16[768,256]{1,0:T(8,128)(2,1)S(1)}, bf16[64,768]{1,0:T(8,128)(2,1)S(1)}, bf16[64,768]{1,0:T(8,128)(2,1)S(1...) custom-call(s32[1]{0:T(128)} %bitcast.core_ref, ...), custom_call_target="tpu_custom_call" | custom-call | flops 19549999104 | tf_op jit(solution)/shard_map/window/pallas_call | solution.py:468
  39.2 0.3 collective-permute-start.3
  39.5 5.4 %table.1.pack_ref = bf16[64,384]{1,0:T(8,128)(2,1)S(1)} custom-call(f32[2,512]{1,0:T(2,128)S(1)} %copy-done.7, f32[1,512]{1,0:T(1,128)S(1)} %bitcast.13, f32[24,512]{1,0:T(8,128)S(1)} %bitcast.11, f32[24,16,512]{2,1,0:T(8,128)S(1)} %get-tuple-element.50.table_ref, f32[1,768]{1,0:T(1,128)S(1)} %get-tuple-element.51.gain_ref, ...), custom_call_target="tpu_custom_call" | custom-call | flops 5750000128 | tf_op jit(solution)/shard_map/table/pallas_call | solution.py:503
  44.9 0.6 collective-permute-start.4
  45.5 0.9 collective-permute-done.4.got_pack_ref
  46.5 0.0 collective-permute-done.3.got_ref
  46.5 2.1 %grads.1 = bf16[16,200,384]{2,1,0:T(8,128)(2,1)S(1)} custom-call(bf16[768,256]{1,0:T(8,128)(2,1)S(1)} %get-tuple-element.48.keep_ref, bf16[3840,256]{1,0:T(8,128)(2,1)S(1)} %get-tuple-element.49.send_ref, bf16[3840,256]{1,0:T(8,128)(2,1)S(1)} %collective-permute-done.3.got_ref, bf16[64,384]{1,0:T(8,128)(2,1)S(1)} %table.1.pack_ref, ...), custom_call_target="tpu_custom_call" | custom-call | flops 2300000000 | tf_op jit(solution)/shard_map/grads/pallas_call | solution.py:521
  48.5 38.3 %all_to_all.15.in_ref = bf16[16,200,384]{2,1,0:T(8,128)(2,1)S(1)} all-to-all(bf16[16,200,384]{2,1,0:T(8,128)(2,1)S(1)} %grads.1), channel_id=1, replica_groups={{0,32,64,96,128,160,192,224,16,48,80,112,144,176,208,240},{1,33,65,97,1..., dimensions={0} | all-to-all | bytes 4915200 | tf_op jit(solution)/shard_map/all_to_all | solution.py:418
  86.8 1.0 plane.1
  87.8 6.6 %all-to-all-start.1 = ((bf16[8,32,384]{2,1,0:T(8,128)(2,1)}), bf16[8,32,384]{2,1,0:T(8,128)(2,1)S(1)}, u32[]{:S(2)}, u32[]{:S(2)}) async-start(bf16[8,32,384]{2,1,0:T(8,128)(2,1)} %plane.1), calls=%async_computation.1 | async-start | bytes 393216 | tf_op jit(solution)/shard_map/all_to_all | solution.py:418
  94.4 0.0 collective-permute-start.5
  94.5 0.3 collective-permute-start.6
  94.8 1.9 %collective-permute-start.7 = (bf16[64,768]{1,0:T(8,128)(2,1)S(1)}, bf16[64,768]{1,0:T(8,128)(2,1)S(1)}, u32[]{:S(2)}, u32[]{:S(2)}) collective-permute-start(bf16[64,768]{1,0:T(8,128)(2,1)S(1)} %get-tuple-element.61), channel_id=1, source_target_pairs={{0,33},{1,34},{2,35},{3,36},{4,37},{5,38},{6,39},{7,40},{8,41},{9,... | collective-permute-start | bytes 294920 | tf_op jit(solution)/shard_map/ppermute | solution.py:542
  96.7 6.7 %collective-permute-done.5 = bf16[64,768]{1,0:T(8,128)(2,1)S(1)} collective-permute-done((bf16[64,768]{1,0:T(8,128)(2,1)S(1)}, bf16[64,768]{1,0:T(8,128)(2,1)S(1)}, u32[]{:S(2)}, u32[]{:S(2)}) %collective-permute-start.5) | collective-permute-done | bytes 98336 | tf_op jit(solution)/shard_map/ppermute | solution.py:542
  103.4 0.0 collective-permute-done.6
  103.4 0.4 collective-permute-done.7
  103.8 1.5 %all-to-all-done.1.in_ref = bf16[8,32,384]{2,1,0:T(8,128)(2,1)S(1)} async-done(((bf16[8,32,384]{2,1,0:T(8,128)(2,1)}), bf16[8,32,384]{2,1,0:T(8,128)(2,1)S(1)}, u32[]{:S(2)}, u32[]{:S(2)}) %all-to-all-start.1) | async-done | bytes 196640 | tf_op jit(solution)/shard_map/all_to_all | solution.py:418
  105.3 0.7 column.1
  106.1 4.6 %all-to-all-start.2 = ((bf16[8,32,384]{2,1,0:T(8,128)(2,1)}), bf16[8,32,384]{2,1,0:T(8,128)(2,1)S(1)}, u32[]{:S(2)}, u32[]{:S(2)}) async-start(bf16[8,32,384]{2,1,0:T(8,128)(2,1)} %column.1), calls=%async_computation.2 | async-start | bytes 393216 | tf_op jit(solution)/shard_map/all_to_all | solution.py:418
  110.7 0.8 maximum_maximum_fusion
  111.4 5.0 %all-to-all-done.2.in_ref = bf16[8,32,384]{2,1,0:T(8,128)(2,1)S(1)} async-done(((bf16[8,32,384]{2,1,0:T(8,128)(2,1)}), bf16[8,32,384]{2,1,0:T(8,128)(2,1)S(1)}, u32[]{:S(2)}, u32[]{:S(2)}) %all-to-all-start.2) | async-done | bytes 196640 | tf_op jit(solution)/shard_map/all_to_all | solution.py:418
  116.5 0.7 finish.1
Async XLA Ops:
  0.6 1.0 copy-start.2
  1.6 1.0 copy-start.3
  2.6 10.8 %copy-start.4 = (f32[512,24]{0,1:T(8,128)S(1)}, f32[512,24]{0,1:T(8,128)}, u32[]{:S(2)}) copy-start(f32[512,24]{0,1:T(8,128)} %param.18) | copy-start | bytes 147460
  2.6 10.8 %copy-start.5 = (s32[16,16]{1,0:T(8,128)S(1)}, s32[16,16]{1,0:T(8,128)}, u32[]{:S(2)}) copy-start(s32[16,16]{1,0:T(8,128)} %valid_hbm.1) | copy-start | bytes 3076
  2.6 10.8 %copy-start.7 = (f32[2,512]{1,0:T(2,128)S(1)}, f32[2,512]{1,0:T(2,128)}, u32[]{:S(2)}) copy-start(f32[2,512]{1,0:T(2,128)} %inner_hbm.3) | copy-start | bytes 12292
  2.6 10.8 %copy-start.8 = (f32[512]{0:T(512)S(1)}, f32[512]{0:T(512)}, u32[]{:S(2)}) copy-start(f32[512]{0:T(512)} %param.17) | copy-start | bytes 6148
  2.6 10.8 %copy-start.9 = (f32[24]{0:T(128)S(1)}, f32[24]{0:T(128)}, u32[]{:S(2)}) copy-start(f32[24]{0:T(128)} %log_ref.1) | copy-start | bytes 292
  3.1 14.6 %collective-permute-start = (bf16[128,768]{1,0:T(8,128)(2,1)S(1)}, bf16[128,768]{1,0:T(8,128)(2,1)S(1)}, u32[]{:S(2)}, u32[]{:S(2)}) collective-permute-start(bf16[128,768]{1,0:T(8,128)(2,1)S(1)} %get-tuple-element.45), channel_id=1, source_target_pairs={{0,31},{1,0},{2,1},{3,2},{4,3},{5,4},{6,5},{7,6},{8,7},{9,8},{10,9... | collective-permute-start | bytes 589832 | tf_op jit(solution)/shard_map/ppermute | solution.py:437
  10.0 7.8 %collective-permute-start.1 = (bf16[128,768]{1,0:T(8,128)(2,1)S(1)}, bf16[128,768]{1,0:T(8,128)(2,1)S(1)}, u32[]{:S(2)}, u32[]{:S(2)}) collective-permute-start(bf16[128,768]{1,0:T(8,128)(2,1)S(1)} %get-tuple-element.46), channel_id=1, source_target_pairs={{0,224},{1,225},{2,226},{3,227},{4,228},{5,229},{6,230},{7,231},{8... | collective-permute-start | bytes 589832 | tf_op jit(solution)/shard_map/ppermute | solution.py:437
  11.5 7.2 %collective-permute-start.2 = (bf16[128,768]{1,0:T(8,128)(2,1)S(1)}, bf16[128,768]{1,0:T(8,128)(2,1)S(1)}, u32[]{:S(2)}, u32[]{:S(2)}) collective-permute-start(bf16[128,768]{1,0:T(8,128)(2,1)S(1)} %get-tuple-element.47), channel_id=1, source_target_pairs={{0,255},{1,224},{2,225},{3,226},{4,227},{5,228},{6,229},{7,230},{8... | collective-permute-start | bytes 589832 | tf_op jit(solution)/shard_map/ppermute | solution.py:437
  13.5 5.2 %copy-start.1 = (bf16[768,768]{1,0:T(8,128)(2,1)S(1)}, bf16[768,768]{1,0:T(8,128)(2,1)}, u32[]{:S(2)}) copy-start(bf16[768,768]{1,0:T(8,128)(2,1)} %out_weight_hbm.1) | copy-start | bytes 3538948
  13.5 5.2 %copy-start.6 = (f32[768]{0:T(1024)S(1)}, f32[768]{0:T(1024)}, u32[]{:S(2)}) copy-start(f32[768]{0:T(1024)} %gain_hbm.1) | copy-start | bytes 9220
  17.0 0.7 copy-start.10
  18.7 2.0 %copy-start = (bf16[768,2304]{1,0:T(8,128)(2,1)S(1)}, bf16[768,2304]{1,0:T(8,128)(2,1)}, u32[]{:S(2)}) copy-start(bf16[768,2304]{1,0:T(8,128)(2,1)} %weight_hbm.1) | copy-start | bytes 10616836
  20.7 0.9 copy-start.11
  39.2 7.3 %collective-permute-start.3 = (bf16[3840,256]{1,0:T(8,128)(2,1)S(1)}, bf16[3840,256]{1,0:T(8,128)(2,1)S(1)}, u32[]{:S(2)}, u32[]{:S(2)}) collective-permute-start(bf16[3840,256]{1,0:T(8,128)(2,1)S(1)} %get-tuple-element.49.send_ref), channel_id=1, source_target_pairs={{0,1},{1,0},{2,3},{3,2},{4,5},{5,4},{6,7},{7,6},{8,9},{9,8},{10,11... | collective-permute-start | bytes 5898248 | tf_op jit(solution)/shard_map/ppermute | solution.py:502
  44.9 1.5 %collective-permute-start.4 = (bf16[64,384]{1,0:T(8,128)(2,1)S(1)}, bf16[64,384]{1,0:T(8,128)(2,1)S(1)}, u32[]{:S(2)}, u32[]{:S(2)}) collective-permute-start(bf16[64,384]{1,0:T(8,128)(2,1)S(1)} %table.1.pack_ref), channel_id=1, source_target_pairs={{0,1},{1,0},{2,3},{3,2},{4,5},{5,4},{6,7},{7,6},{8,9},{9,8},{10,11... | collective-permute-start | bytes 147464 | tf_op jit(solution)/shard_map/ppermute | solution.py:520
  87.8 17.5 %all-to-all-start.1 = ((bf16[8,32,384]{2,1,0:T(8,128)(2,1)}), bf16[8,32,384]{2,1,0:T(8,128)(2,1)S(1)}, u32[]{:S(2)}, u32[]{:S(2)}) async-start(bf16[8,32,384]{2,1,0:T(8,128)(2,1)} %plane.1), calls=%async_computation.1 | async-start | bytes 393216 | tf_op jit(solution)/shard_map/all_to_all | solution.py:418
  94.4 9.0 %collective-permute-start.5 = (bf16[64,768]{1,0:T(8,128)(2,1)S(1)}, bf16[64,768]{1,0:T(8,128)(2,1)S(1)}, u32[]{:S(2)}, u32[]{:S(2)}) collective-permute-start(bf16[64,768]{1,0:T(8,128)(2,1)S(1)} %get-tuple-element.59), channel_id=1, source_target_pairs={{0,1},{1,2},{2,3},{3,4},{4,5},{5,6},{6,7},{7,8},{8,9},{9,10},{10,1... | collective-permute-start | bytes 294920 | tf_op jit(solution)/shard_map/ppermute | solution.py:542
  94.5 9.0 %collective-permute-start.6 = (bf16[64,768]{1,0:T(8,128)(2,1)S(1)}, bf16[64,768]{1,0:T(8,128)(2,1)S(1)}, u32[]{:S(2)}, u32[]{:S(2)}) collective-permute-start(bf16[64,768]{1,0:T(8,128)(2,1)S(1)} %get-tuple-element.60), channel_id=1, source_target_pairs={{0,32},{1,33},{2,34},{3,35},{4,36},{5,37},{6,38},{7,39},{8,40},{9,... | collective-permute-start | bytes 294920 | tf_op jit(solution)/shard_map/ppermute | solution.py:542
  94.8 9.1 %collective-permute-start.7 = (bf16[64,768]{1,0:T(8,128)(2,1)S(1)}, bf16[64,768]{1,0:T(8,128)(2,1)S(1)}, u32[]{:S(2)}, u32[]{:S(2)}) collective-permute-start(bf16[64,768]{1,0:T(8,128)(2,1)S(1)} %get-tuple-element.61), channel_id=1, source_target_pairs={{0,33},{1,34},{2,35},{3,36},{4,37},{5,38},{6,39},{7,40},{8,41},{9,... | collective-permute-start | bytes 294920 | tf_op jit(solution)/shard_map/ppermute | solution.py:542
  106.1 10.4 %all-to-all-start.2 = ((bf16[8,32,384]{2,1,0:T(8,128)(2,1)}), bf16[8,32,384]{2,1,0:T(8,128)(2,1)S(1)}, u32[]{:S(2)}, u32[]{:S(2)}) async-start(bf16[8,32,384]{2,1,0:T(8,128)(2,1)} %column.1), calls=%async_computation.2 | async-start | bytes 393216 | tf_op jit(solution)/shard_map/all_to_all | solution.py:418

commit v2 on v1

--- a/solution.py
+++ b/solution.py
@@ -48,8 +48,7 @@
 
 def hidden_of(inner_ref, offset_ref):
     first, second = slot_coords()
-    before = first * inner_ref[0:1, :] + second * inner_ref[1:2, :] + offset_ref[...]
-    return first, second, before, jnp.maximum(before, 0.0)
+    return jnp.maximum(first * inner_ref[0:1, :] + second * inner_ref[1:2, :] + offset_ref[...], 0.0)
 
 
 def fetch(pairs, sems, first=0):
@@ -73,23 +72,15 @@
 
 
 def bias_kernel(
-    last_ref, log_ref, inner_hbm, offset_hbm, outer_hbm, valid_hbm,
-    table_ref, mask_ref, factor_ref,
-    inner_ref, offset_ref, outer_ref, valid_ref, rows_ref, in_sems,
+    last_ref, log_ref, inner_ref, offset_ref, outer_ref, valid_ref, gain_ref,
+    table_ref, mask_ref, factor_ref, hidden_ref, slope_ref, gain_out, rows_ref,
 ):
-    for copy in fetch(
-        (
-            (inner_hbm, inner_ref),
-            (offset_hbm, offset_ref),
-            (outer_hbm, outer_ref),
-            (valid_hbm, valid_ref),
-        ),
-        in_sems,
-    ):
-        copy.wait()
-    hidden = hidden_of(inner_ref, offset_ref)[3]
-    logits = mm(outer_ref[...], hidden, NT, exact)
-    grid = 16.0 * jax.nn.sigmoid(logits)
+    gain_out[...] = gain_ref[...].reshape(1, D)
+    hidden = hidden_of(inner_ref, offset_ref)
+    hidden_ref[...] = hidden
+    sig = jax.nn.sigmoid(mm(outer_ref[...], hidden, NT, exact))
+    grid = 16.0 * sig
+    slope_ref[...] = grid * (1.0 - sig)
     even = grid[:, :512]
     odd = grid[:, 512:]
     lane = lax.broadcasted_iota(jnp.int32, (HEADS, 512), 1)
@@ -115,25 +106,10 @@
 
 
 def window_kernel(
-    core_ref, factor_ref, table_ref, mask_ref, q00, q01, q10, q11, gain_hbm, weight_hbm, out_weight_hbm,
+    core_ref, factor_ref, table_ref, mask_ref, q00, q01, q10, q11, gain_ref, weight_ref, out_weight_ref,
     send_ref, keep_ref, d00, d01, d10, d11, gain_out, scale_out, table_out,
-    grid3, up, tokt, projt, exps, inv, hot, doutt, weight_ref, out_weight_ref, gain_ref, sems,
+    grid3, up, tokt, projt, exps, inv, hot, doutt, means,
 ):
-    weight_copies = [
-        pltpu.make_async_copy(
-            weight_hbm.at[:, part * PART : (part + 1) * PART],
-            weight_ref.at[:, part * PART : (part + 1) * PART],
-            sems.at[part],
-        )
-        for part in range(6)
-    ]
-    out_weight_copy = pltpu.make_async_copy(out_weight_hbm, out_weight_ref, sems.at[6])
-    gain_copy = pltpu.make_async_copy(gain_hbm, gain_ref, sems.at[7])
-    for copy in weight_copies:
-        copy.start()
-    gain_copy.start()
-    out_weight_copy.start()
-
     places = ((0, 0), (0, 8), (8, 0), (8, 8))
     quads = (q00, q01, q10, q11)
 
@@ -157,7 +133,6 @@
     tokt[...] = tokens32.T
     for part in range(6):
         cols = slice(part * PART, (part + 1) * PART)
-        weight_copies[part].wait()
         projt[cols, :] = mm(tokens, weight_ref[:, cols]).T
     keep_ref[0:384, :] = rows_of(tokt, mine)
     send_ref[0:384, :] = rows_of(tokt, 1 - mine)
@@ -192,9 +167,10 @@
         weights = jnp.concatenate(slabs, 0)
         exps[head] = weights
         values = jnp.concatenate([v, jnp.where(extra == 0, 1.0, 0.0)], 0).astype(bf16)
-        mixed = mm(values, weights)
+        mixed = mm(jnp.concatenate([values, k_round], 0), weights)
         inverse = 1.0 / mixed[HEAD_DIM : HEAD_DIM + 1, :]
         inv[head] = inverse
+        means[head] = jnp.sum(q_round.astype(f32) * mixed[48:, :], 0, keepdims=True) * inverse
         hot[pl.ds(at, HEAD_DIM), :] = mixed[:HEAD_DIM, :] * inverse
         return carry
 
@@ -202,8 +178,6 @@
 
     keep_ref[384:768, :] = rows_of(hot, mine)
     send_ref[384:768, :] = rows_of(hot, 1 - mine)
-    out_weight_copy.wait()
-    gain_copy.wait()
     heads_out = hot[...].T.astype(bf16)
     mixed_out = mm(heads_out, out_weight_ref[...])
     centre = jnp.mean(mixed_out, -1, keepdims=True)
@@ -212,7 +186,7 @@
     normed = shifted * inverse
     up_now = up[...]
     gain_out[...] = jnp.sum(up_now * normed, 0, keepdims=True)
-    dnormed = up_now * gain_ref[...].reshape(1, D)
+    dnormed = up_now * gain_ref[...]
     dmixed = (
         dnormed
         - jnp.mean(dnormed, -1, keepdims=True)
@@ -236,9 +210,14 @@
         dscores = weights.astype(f32) * mm(values, dout_more, TN)
         dround = dscores.astype(bf16)
         dvalue = mm(dout.astype(bf16), weights, NT)
-        dquery = mm(k_round, dround)
+        ones = jnp.where(extra == 0, 1.0, 0.0).astype(bf16)
+        dquery = mm(jnp.concatenate([k_round, ones], 0), dround)
+        excess = dquery[HEAD_DIM : HEAD_DIM + 1, :]
+        dquery = dquery[:HEAD_DIM, :]
         dkey = mm(q_round, dround, NT)
-        scale_out[pl.ds(head, 1), :] = jnp.sum(dscores * mm(k_round, q_round, TN), 0, keepdims=True)
+        scale_out[pl.ds(head, 1), :] = (
+            jnp.sum(q_round.astype(f32) * dquery, 0, keepdims=True) - means[head] * excess
+        )
         dquery = dquery * factor
         dquery = (dquery - q_unit * jnp.sum(q_unit * dquery, 0, keepdims=True)) * q_inv
         dkey = (dkey - k_unit * jnp.sum(k_unit * dkey, 0, keepdims=True)) * k_inv
@@ -266,16 +245,9 @@
         part[...] = grid3[r : r + 8, c : c + 8, :].reshape(QUAD, D).astype(bf16)
 
 
-def table_kernel(
-    inner_hbm, offset_hbm, outer_hbm, table_ref, gain_ref, scale_ref,
-    pack_ref,
-    inner_ref, offset_ref, outer_ref, rows_ref, work_ref, sems,
-):
-    for copy in fetch(((inner_hbm, inner_ref), (offset_hbm, offset_ref), (outer_hbm, outer_ref)), sems):
-        copy.wait()
-    first_coord, second_coord, before, hidden = hidden_of(inner_ref, offset_ref)
-    logits = mm(outer_ref[...], hidden, NT, exact)
-    sig = jax.nn.sigmoid(logits)
+def table_kernel(outer_ref, hidden_ref, slope_ref, table_ref, gain_ref, scale_ref, pack_ref, rows_ref, work_ref):
+    first_coord, second_coord = slot_coords()
+    hidden = hidden_ref[...]
     lane = lax.broadcasted_iota(jnp.int32, (HEADS, 512), 1)
     first = (lane % 32) < 16
     for head in range(HEADS):
@@ -287,10 +259,10 @@
         even = even + pltpu.roll(jnp.where(first, row, 0.0), 15 - cj, 1)
         odd = odd + pltpu.roll(jnp.where(first, 0.0, row), (512 - 1 - cj) % 512, 1)
     dgrid = jnp.concatenate([even, odd], 1)
-    dlogits = 16.0 * dgrid * sig * (1.0 - sig)
+    dlogits = dgrid * slope_ref[...]
     outer = mm(dlogits, hidden, NN, exact)
     dhidden = mm(dlogits, outer_ref[...], TN, exact)
-    dhidden = jnp.where(before > 0.0, dhidden, 0.0)
+    dhidden = jnp.where(hidden > 0.0, dhidden, 0.0)
     scale = jnp.sum(scale_ref[...], -1, keepdims=True)
     where_row = lax.broadcasted_iota(jnp.int32, (HEADS, PART), 0)
     where_lane = lax.broadcasted_iota(jnp.int32, (HEADS, PART), 1)
@@ -442,27 +414,23 @@
     offset_row = table_offset.reshape(1, HIDDEN)
     last = (lax.axis_index("lat") == lax.axis_size("lat") - 1).astype(jnp.int32).reshape(1)
     core = (lax.axis_index("lon") % 2).astype(jnp.int32).reshape(1)
-    bias, mask, factor = pl.pallas_call(
+    bias, mask, factor, hidden, slope, gain_row = pl.pallas_call(
         bias_kernel,
         out_shape=(
             jax.ShapeDtypeStruct((HEADS, WIN, 512), f32),
             jax.ShapeDtypeStruct((AREA, AREA), f32),
             jax.ShapeDtypeStruct((HEADS, 1, AREA), f32),
+            jax.ShapeDtypeStruct((SLOTS, HIDDEN), f32),
+            jax.ShapeDtypeStruct((HEADS, SLOTS), f32),
+            jax.ShapeDtypeStruct((1, D), f32),
         ),
-        in_specs=[SMEM] * 2 + [HBM] * 4,
-        out_specs=tuple(vmem(3)),
-        scratch_shapes=[
-            pltpu.VMEM((2, HIDDEN), f32),
-            pltpu.VMEM((1, HIDDEN), f32),
-            pltpu.VMEM((HEADS, HIDDEN), f32),
-            pltpu.VMEM((WIN, WIN), jnp.int32),
-            pltpu.VMEM((WIN, HEADS, 512), f32),
-            pltpu.SemaphoreType.DMA((4,)),
-        ],
+        in_specs=[SMEM] * 2 + vmem(5),
+        out_specs=tuple(vmem(6)),
+        scratch_shapes=[pltpu.VMEM((WIN, HEADS, 512), f32)],
         compiler_params=params(16),
-        cost_estimate=cost(30),
+        cost_estimate=cost(2),
         name="bias",
-    )(last, logit_scale, table_inner, offset_row, outer_t, validity)
+    )(last, logit_scale, table_inner, offset_row, outer_t, validity, norm_gain)
 
     quad_shape = jax.ShapeDtypeStruct((QUAD, D), bf16)
     send, keep, *dquads, gain_part, scale_part, table_part = pl.pallas_call(
@@ -478,7 +446,7 @@
             jax.ShapeDtypeStruct((HEADS, AREA), f32),
             jax.ShapeDtypeStruct((HEADS, WIN, 512), f32),
         ),
-        in_specs=[SMEM] + vmem(7) + [HBM] * 3,
+        in_specs=[SMEM] + vmem(10),
         out_specs=tuple(vmem(9)),
         scratch_shapes=[
             pltpu.VMEM((WIN, WIN, D), f32),
@@ -489,34 +457,24 @@
             pltpu.VMEM((HEADS, 1, AREA), f32),
             pltpu.VMEM((D, AREA), f32),
             pltpu.VMEM((D, AREA), bf16),
-            pltpu.VMEM((D, 3 * D), bf16),
-            pltpu.VMEM((D, D), bf16),
-            pltpu.VMEM((D,), f32),
-            pltpu.SemaphoreType.DMA((8,)),
+            pltpu.VMEM((HEADS, 1, AREA), f32),
         ],
         compiler_params=params(36),
         cost_estimate=cost(17),
         name="window",
-    )(core, factor, bias, mask, *moved, norm_gain, attend_weight, output_weight)
+    )(core, factor, bias, mask, *moved, gain_row, attend_weight, output_weight)
 
     got = lax.ppermute(send, BOTH, CORES)
     pack = pl.pallas_call(
         table_kernel,
         out_shape=jax.ShapeDtypeStruct((64, PART), bf16),
-        in_specs=[HBM] * 3 + vmem(3),
+        in_specs=vmem(6),
         out_specs=vmem(1)[0],
-        scratch_shapes=[
-            pltpu.VMEM((2, HIDDEN), f32),
-            pltpu.VMEM((1, HIDDEN), f32),
-            pltpu.VMEM((HEADS, HIDDEN), f32),
-            pltpu.VMEM((WIN, HEADS, 512), f32),
-            pltpu.VMEM((64, PART), f32),
-            pltpu.SemaphoreType.DMA((3,)),
-        ],
+        scratch_shapes=[pltpu.VMEM((WIN, HEADS, 512), f32), pltpu.VMEM((64, PART), f32)],
         compiler_params=params(16),
         cost_estimate=cost(5),
         name="table",
-    )(table_inner, offset_row, outer_t, table_part, gain_part, scale_part)
+    )(outer_t, hidden, slope, table_part, gain_part, scale_part)
     got_pack = lax.ppermute(pack, BOTH, CORES)
     grads = pl.pallas_call(
         grads_kernel,
@@ -558,6 +516,7 @@
     input_delta = jnp.concatenate(
         [jnp.concatenate([back[3], back[2]], 1), jnp.concatenate([back[1], back[0]], 1)], 0
     )
+    column, input_delta = lax.optimization_barrier((column, input_delta))
 
     attend_delta, output_delta, gain, scale, inner, offset, outer = pl.pallas_call(
         finish_kernel,

time: 118 us -> 110 us (0.932)
  blocking collectives: 38.3 us -> 47.9 us
  starting transfers between devices: 24.7 us -> 20.1 us
  Pallas kernels: 31.4 us -> 27 us
  waiting for transfers between devices: 15.6 us -> 11.4 us
  local copies, waits for them, and re-layouts: 5.66 us -> 2.02 us
    all_to_all x1 -> x2, blocking collectives: 38.3 us -> 47.9 us  [exchange(): lax.all_to_all(value, BOTH, 0, 0, axis_index_groups=groups, tiled=True)]
    all_to_all x2 -> x1, waiting for transfers between devices: 6.52 us -> 1.5 us  [exchange(): lax.all_to_all(value, BOTH, 0, 0, axis_index_groups=groups, tiled=True)]
    all_to_all x2 -> x1, starting transfers between devices: 11.2 us -> 6.63 us  [exchange(): lax.all_to_all(value, BOTH, 0, 0, axis_index_groups=groups, tiled=True)]
    unnamed x24 -> x20, local copies, waits for them, and re-layouts: 5.66 us -> 2.02 us
    pallas_call x1, Pallas kernels: 17.5 us -> 15.7 us  [per_device(): pl.pallas_call(window_kernel, out_shape=(jax.ShapeDtypeStruct((3840, AREA...]
    pallas_call x1, Pallas kernels: 5.43 us -> 3.76 us  [per_device(): pl.pallas_call(table_kernel, out_shape=jax.ShapeDtypeStruct((64, PART), b...]
  transfers between devices with their start and end apart: 10 -> 9, of which waited for: 7 -> 6; matrix products, arithmetic and copies ran while one was open for 1% -> 0% of each run, Pallas kernels for 8% -> 6%
where the time goes in v2:
time: 110 us
  blocking collectives  47.9 us (44%)
  Pallas kernels  27 us (25%)
  starting transfers between devices  20.1 us (18%)
  waiting for transfers between devices  11.4 us (10%)
  local copies, waits for them, and re-layouts  2.02 us (2%)
    all_to_all x2, blocking collectives, exchange(): lax.all_to_all(value, BOTH, 0, 0, axis_index_groups=groups, tiled=True)  47.9 us
    pallas_call x1, Pallas kernels, per_device(): pl.pallas_call(window_kernel, out_shape=(jax.ShapeDtypeStruct((3840, AREA...  15.7 us
    ppermute x3, starting transfers between devices, per_device(): lax.ppermute(value, BOTH, shift_pairs(-step[0], -step[1]))  10.3 us
    ppermute x3, waiting for transfers between devices, per_device(): lax.ppermute(value, BOTH, shift_pairs(*step))  7.15 us
    all_to_all x1, starting transfers between devices, exchange(): lax.all_to_all(value, BOTH, 0, 0, axis_index_groups=groups, tiled=True)  6.63 us
    pallas_call x1, Pallas kernels, per_device(): pl.pallas_call(table_kernel, out_shape=jax.ShapeDtypeStruct((64, PART), b...  3.76 us
    pallas_call x1, Pallas kernels, per_device(): pl.pallas_call(bias_kernel, out_shape=(jax.ShapeDtypeStruct((HEADS, WIN,...  3.31 us
    ppermute x3, starting transfers between devices, per_device(): lax.ppermute(value, BOTH, shift_pairs(*step))  2.24 us
  transfers between devices with their start and end apart: 9, of which 6 were waited for; matrix products, arithmetic and copies ran while one was open for 0% of the time, Pallas kernels for 6%

profile of v2, /device:TPU:2, one launch (start us, length us, event | category | flops | bytes accessed | tf_op | source)
XLA Modules:
  0.0 110.0 jit_solution(1845286601880629568)
XLA Ops:
  0.6 0.0 copy-start.2
  0.6 1.0 copy-done.2
  1.6 0.0 copy-start.3
  1.6 1.0 copy-done.3
  2.6 0.0 copy-start.4
  2.6 0.0 copy-start.5
  2.6 0.0 copy-start.6
  2.6 0.0 copy-start.7
  2.6 0.0 copy-start.8
  2.6 0.0 copy-start.9
  2.7 0.4 cut.1
  3.1 6.9 %collective-permute-start = (bf16[128,768]{1,0:T(8,128)(2,1)S(1)}, bf16[128,768]{1,0:T(8,128)(2,1)S(1)}, u32[]{:S(2)}, u32[]{:S(2)}) collective-permute-start(bf16[128,768]{1,0:T(8,128)(2,1)S(1)} %get-tuple-element.50), channel_id=1, source_target_pairs={{0,31},{1,0},{2,1},{3,2},{4,3},{5,4},{6,5},{7,6},{8,7},{9,8},{10,9... | collective-permute-start | bytes 589832 | tf_op jit(solution)/shard_map/ppermute | solution.py:409
  10.0 1.4 %collective-permute-start.1 = (bf16[128,768]{1,0:T(8,128)(2,1)S(1)}, bf16[128,768]{1,0:T(8,128)(2,1)S(1)}, u32[]{:S(2)}, u32[]{:S(2)}) collective-permute-start(bf16[128,768]{1,0:T(8,128)(2,1)S(1)} %get-tuple-element.51), channel_id=1, source_target_pairs={{0,224},{1,225},{2,226},{3,227},{4,228},{5,229},{6,230},{7,231},{8... | collective-permute-start | bytes 589832 | tf_op jit(solution)/shard_map/ppermute | solution.py:409
  11.5 2.0 %collective-permute-start.2 = (bf16[128,768]{1,0:T(8,128)(2,1)S(1)}, bf16[128,768]{1,0:T(8,128)(2,1)S(1)}, u32[]{:S(2)}, u32[]{:S(2)}) collective-permute-start(bf16[128,768]{1,0:T(8,128)(2,1)S(1)} %get-tuple-element.52), channel_id=1, source_target_pairs={{0,255},{1,224},{2,225},{3,226},{4,227},{5,228},{6,229},{7,230},{8... | collective-permute-start | bytes 589832 | tf_op jit(solution)/shard_map/ppermute | solution.py:409
  13.5 0.0 copy-done.4
  13.5 0.0 copy-done.5
  13.5 0.0 copy-done.6
  13.5 0.0 copy-done.7
  13.5 0.0 copy-done.8
  13.5 0.0 copy-done.9
  13.5 0.0 copy-start
  13.5 0.0 copy-start.1
  13.5 3.3 %bias.1 = (f32[24,16,512]{2,1,0:T(8,128)S(1)}, f32[256,256]{1,0:T(8,128)S(1)}, f32[24,1,256]{2,1,0:T(1,128)S(1)}, f32[1024,512]{1,0:T(8,128)S(1)}, f32[24,1024]{1,0:T(8,128)S(1)}, /*index=5*/f32[1,768]{1,0:T(1,128)S(1)}) custom-call(s32[1]{0:T(128)} %bitcast.1.last_ref, f32[24]{0:T(128)S(1)} %copy-done.9, f32[2,512]{1,0:T(2,128)S(1)} %copy-done.6, ...), custom_call_target="tpu_custom_call" | custom-call | flops 2300000000 | tf_op jit(solution)/shard_map/bias/pallas_call | solution.py:417
  16.8 0.0 collective-permute-done.q01
  16.8 1.0 collective-permute-done.1.q10
  17.9 0.8 collective-permute-done.2.q11
  18.7 0.0 copy-done
  18.7 0.0 copy-done.1
  18.7 15.7 %window.1 = (bf16[3840,256]{1,0:T(8,128)(2,1)S(1)}, bf16[768,256]{1,0:T(8,128)(2,1)S(1)}, bf16[64,768]{1,0:T(8,128)(2,1)S(1)}, bf16[64,768]{1,0:T(8,128)(2,1)S(1...) custom-call(s32[1]{0:T(128)} %bitcast.core_ref, ...), custom_call_target="tpu_custom_call" | custom-call | flops 19549999104 | tf_op jit(solution)/shard_map/window/pallas_call | solution.py:436
  34.4 0.1 collective-permute-start.3
  34.5 3.8 %table.1.pack_ref = bf16[64,384]{1,0:T(8,128)(2,1)S(1)} custom-call(f32[24,512]{1,0:T(8,128)S(1)} %bitcast.11, f32[1024,512]{1,0:T(8,128)S(1)} %get-tuple-element.56.hidden_ref, f32[24,1024]{1,0:T(8,128)S(1)} %get-tuple-element.57.slope_ref, f32[24,16,512]{2,1,0:T(8,128)S(1)} %get-tuple-element.58.table_ref, f32[1,768]{1,0:T(1,128)S(1)} %get-tuple-element.59.gain_ref, ...), custom_call_target="tpu_custom_call" | custom-call | flops 5750000128 | tf_op jit(solution)/shard_map/table/pallas_call | solution.py:468
  38.3 0.8 collective-permute-start.4
  39.1 0.9 collective-permute-done.4.got_pack_ref
  40.0 0.0 collective-permute-done.3.got_ref
  40.0 2.1 %grads.1 = bf16[16,200,384]{2,1,0:T(8,128)(2,1)S(1)} custom-call(bf16[768,256]{1,0:T(8,128)(2,1)S(1)} %get-tuple-element.54.keep_ref, bf16[3840,256]{1,0:T(8,128)(2,1)S(1)} %get-tuple-element.55.send_ref, bf16[3840,256]{1,0:T(8,128)(2,1)S(1)} %collective-permute-done.3.got_ref, bf16[64,384]{1,0:T(8,128)(2,1)S(1)} %table.1.pack_ref, ...), custom_call_target="tpu_custom_call" | custom-call | flops 2300000000 | tf_op jit(solution)/shard_map/grads/pallas_call | solution.py:479
  42.0 38.3 %all_to_all.15.in_ref = bf16[16,200,384]{2,1,0:T(8,128)(2,1)S(1)} all-to-all(bf16[16,200,384]{2,1,0:T(8,128)(2,1)S(1)} %grads.1), channel_id=1, replica_groups={{0,32,64,96,128,160,192,224,16,48,80,112,144,176,208,240},{1,33,65,97,1..., dimensions={0} | all-to-all | bytes 4915200 | tf_op jit(solution)/shard_map/all_to_all | solution.py:390
  80.4 1.0 plane.1
  81.4 6.6 %all-to-all-start.1 = ((bf16[8,32,384]{2,1,0:T(8,128)(2,1)}), bf16[8,32,384]{2,1,0:T(8,128)(2,1)S(1)}, u32[]{:S(2)}, u32[]{:S(2)}) async-start(bf16[8,32,384]{2,1,0:T(8,128)(2,1)} %plane.1), calls=%async_computation.1 | async-start | bytes 393216 | tf_op jit(solution)/shard_map/all_to_all | solution.py:390
  88.0 0.0 collective-permute-start.5
  88.0 0.3 collective-permute-start.6
  88.3 1.9 %collective-permute-start.7 = (bf16[64,768]{1,0:T(8,128)(2,1)S(1)}, bf16[64,768]{1,0:T(8,128)(2,1)S(1)}, u32[]{:S(2)}, u32[]{:S(2)}) collective-permute-start(bf16[64,768]{1,0:T(8,128)(2,1)S(1)} %get-tuple-element.69), channel_id=1, source_target_pairs={{0,33},{1,34},{2,35},{3,36},{4,37},{5,38},{6,39},{7,40},{8,41},{9,... | collective-permute-start | bytes 294920 | tf_op jit(solution)/shard_map/ppermute | solution.py:500
  90.2 6.7 %collective-permute-done.5 = bf16[64,768]{1,0:T(8,128)(2,1)S(1)} collective-permute-done((bf16[64,768]{1,0:T(8,128)(2,1)S(1)}, bf16[64,768]{1,0:T(8,128)(2,1)S(1)}, u32[]{:S(2)}, u32[]{:S(2)}) %collective-permute-start.5) | collective-permute-done | bytes 98336 | tf_op jit(solution)/shard_map/ppermute | solution.py:500
  97.0 0.0 collective-permute-done.6
  97.0 0.4 collective-permute-done.7
  97.4 1.5 %all-to-all-done.1.in_ref = bf16[8,32,384]{2,1,0:T(8,128)(2,1)S(1)} async-done(((bf16[8,32,384]{2,1,0:T(8,128)(2,1)}), bf16[8,32,384]{2,1,0:T(8,128)(2,1)S(1)}, u32[]{:S(2)}, u32[]{:S(2)}) %all-to-all-start.1) | async-done | bytes 196640 | tf_op jit(solution)/shard_map/all_to_all | solution.py:390
  98.9 0.8 maximum_maximum_fusion
  99.7 9.5 %all_to_all.16.in_ref = bf16[8,32,384]{2,1,0:T(8,128)(2,1)S(1)} all-to-all(bf16[8,32,384]{2,1,0:T(8,128)(2,1)S(1)} %column.1), channel_id=1, replica_groups={{0,32,64,96,128,160,192,224},{1,33,65,97,129,161,193,225},{2,34,66,98,1..., dimensions={0} | all-to-all | bytes 393216 | tf_op jit(solution)/shard_map/all_to_all | solution.py:390
  109.2 0.7 finish.1
  (1 shorter events, 0.0 us)
Async XLA Ops:
  0.6 1.0 copy-start.2
  1.6 1.0 copy-start.3
  2.6 10.8 %copy-start.4 = (f32[512,24]{0,1:T(8,128)S(1)}, f32[512,24]{0,1:T(8,128)}, u32[]{:S(2)}) copy-start(f32[512,24]{0,1:T(8,128)} %param.18) | copy-start | bytes 147460
  2.6 10.8 %copy-start.5 = (s32[16,16]{1,0:T(8,128)S(1)}, s32[16,16]{1,0:T(8,128)}, u32[]{:S(2)}) copy-start(s32[16,16]{1,0:T(8,128)} %valid_ref.1) | copy-start | bytes 3076
  2.6 10.8 %copy-start.6 = (f32[2,512]{1,0:T(2,128)S(1)}, f32[2,512]{1,0:T(2,128)}, u32[]{:S(2)}) copy-start(f32[2,512]{1,0:T(2,128)} %inner_ref.1) | copy-start | bytes 12292
  2.6 10.8 %copy-start.7 = (f32[768]{0:T(1024)S(1)}, f32[768]{0:T(1024)}, u32[]{:S(2)}) copy-start(f32[768]{0:T(1024)} %gain_ref.1) | copy-start | bytes 9220
  2.6 10.8 %copy-start.8 = (f32[512]{0:T(512)S(1)}, f32[512]{0:T(512)}, u32[]{:S(2)}) copy-start(f32[512]{0:T(512)} %param.17) | copy-start | bytes 6148
  2.6 10.8 %copy-start.9 = (f32[24]{0:T(128)S(1)}, f32[24]{0:T(128)}, u32[]{:S(2)}) copy-start(f32[24]{0:T(128)} %log_ref.1) | copy-start | bytes 292
  3.1 13.7 %collective-permute-start = (bf16[128,768]{1,0:T(8,128)(2,1)S(1)}, bf16[128,768]{1,0:T(8,128)(2,1)S(1)}, u32[]{:S(2)}, u32[]{:S(2)}) collective-permute-start(bf16[128,768]{1,0:T(8,128)(2,1)S(1)} %get-tuple-element.50), channel_id=1, source_target_pairs={{0,31},{1,0},{2,1},{3,2},{4,3},{5,4},{6,5},{7,6},{8,7},{9,8},{10,9... | collective-permute-start | bytes 589832 | tf_op jit(solution)/shard_map/ppermute | solution.py:409
  10.0 7.8 %collective-permute-start.1 = (bf16[128,768]{1,0:T(8,128)(2,1)S(1)}, bf16[128,768]{1,0:T(8,128)(2,1)S(1)}, u32[]{:S(2)}, u32[]{:S(2)}) collective-permute-start(bf16[128,768]{1,0:T(8,128)(2,1)S(1)} %get-tuple-element.51), channel_id=1, source_target_pairs={{0,224},{1,225},{2,226},{3,227},{4,228},{5,229},{6,230},{7,231},{8... | collective-permute-start | bytes 589832 | tf_op jit(solution)/shard_map/ppermute | solution.py:409
  11.5 7.2 %collective-permute-start.2 = (bf16[128,768]{1,0:T(8,128)(2,1)S(1)}, bf16[128,768]{1,0:T(8,128)(2,1)S(1)}, u32[]{:S(2)}, u32[]{:S(2)}) collective-permute-start(bf16[128,768]{1,0:T(8,128)(2,1)S(1)} %get-tuple-element.52), channel_id=1, source_target_pairs={{0,255},{1,224},{2,225},{3,226},{4,227},{5,228},{6,229},{7,230},{8... | collective-permute-start | bytes 589832 | tf_op jit(solution)/shard_map/ppermute | solution.py:409
  13.5 5.2 %copy-start = (bf16[768,2304]{1,0:T(8,128)(2,1)S(1)}, bf16[768,2304]{1,0:T(8,128)(2,1)}, u32[]{:S(2)}) copy-start(bf16[768,2304]{1,0:T(8,128)(2,1)} %weight_ref.1) | copy-start | bytes 10616836
  13.5 5.2 %copy-start.1 = (bf16[768,768]{1,0:T(8,128)(2,1)S(1)}, bf16[768,768]{1,0:T(8,128)(2,1)}, u32[]{:S(2)}) copy-start(bf16[768,768]{1,0:T(8,128)(2,1)} %out_weight_ref.1) | copy-start | bytes 3538948
  34.4 5.5 %collective-permute-start.3 = (bf16[3840,256]{1,0:T(8,128)(2,1)S(1)}, bf16[3840,256]{1,0:T(8,128)(2,1)S(1)}, u32[]{:S(2)}, u32[]{:S(2)}) collective-permute-start(bf16[3840,256]{1,0:T(8,128)(2,1)S(1)} %get-tuple-element.55.send_ref), channel_id=1, source_target_pairs={{0,1},{1,0},{2,3},{3,2},{4,5},{5,4},{6,7},{7,6},{8,9},{9,8},{10,11... | collective-permute-start | bytes 5898248 | tf_op jit(solution)/shard_map/ppermute | solution.py:467
  38.3 1.7 %collective-permute-start.4 = (bf16[64,384]{1,0:T(8,128)(2,1)S(1)}, bf16[64,384]{1,0:T(8,128)(2,1)S(1)}, u32[]{:S(2)}, u32[]{:S(2)}) collective-permute-start(bf16[64,384]{1,0:T(8,128)(2,1)S(1)} %table.1.pack_ref), channel_id=1, source_target_pairs={{0,1},{1,0},{2,3},{3,2},{4,5},{5,4},{6,7},{7,6},{8,9},{9,8},{10,11... | collective-permute-start | bytes 147464 | tf_op jit(solution)/shard_map/ppermute | solution.py:478
  81.4 17.5 %all-to-all-start.1 = ((bf16[8,32,384]{2,1,0:T(8,128)(2,1)}), bf16[8,32,384]{2,1,0:T(8,128)(2,1)S(1)}, u32[]{:S(2)}, u32[]{:S(2)}) async-start(bf16[8,32,384]{2,1,0:T(8,128)(2,1)} %plane.1), calls=%async_computation.1 | async-start | bytes 393216 | tf_op jit(solution)/shard_map/all_to_all | solution.py:390
  88.0 9.0 %collective-permute-start.5 = (bf16[64,768]{1,0:T(8,128)(2,1)S(1)}, bf16[64,768]{1,0:T(8,128)(2,1)S(1)}, u32[]{:S(2)}, u32[]{:S(2)}) collective-permute-start(bf16[64,768]{1,0:T(8,128)(2,1)S(1)} %get-tuple-element.67), channel_id=1, source_target_pairs={{0,1},{1,2},{2,3},{3,4},{4,5},{5,6},{6,7},{7,8},{8,9},{9,10},{10,1... | collective-permute-start | bytes 294920 | tf_op jit(solution)/shard_map/ppermute | solution.py:500
  88.0 9.0 %collective-permute-start.6 = (bf16[64,768]{1,0:T(8,128)(2,1)S(1)}, bf16[64,768]{1,0:T(8,128)(2,1)S(1)}, u32[]{:S(2)}, u32[]{:S(2)}) collective-permute-start(bf16[64,768]{1,0:T(8,128)(2,1)S(1)} %get-tuple-element.68), channel_id=1, source_target_pairs={{0,32},{1,33},{2,34},{3,35},{4,36},{5,37},{6,38},{7,39},{8,40},{9,... | collective-permute-start | bytes 294920 | tf_op jit(solution)/shard_map/ppermute | solution.py:500
  88.3 9.1 %collective-permute-start.7 = (bf16[64,768]{1,0:T(8,128)(2,1)S(1)}, bf16[64,768]{1,0:T(8,128)(2,1)S(1)}, u32[]{:S(2)}, u32[]{:S(2)}) collective-permute-start(bf16[64,768]{1,0:T(8,128)(2,1)S(1)} %get-tuple-element.69), channel_id=1, source_target_pairs={{0,33},{1,34},{2,35},{3,36},{4,37},{5,38},{6,39},{7,40},{8,41},{9,... | collective-permute-start | bytes 294920 | tf_op jit(solution)/shard_map/ppermute | solution.py:500

commit v3 on v2

--- a/solution.py
+++ b/solution.py
@@ -107,7 +107,7 @@
 
 def window_kernel(
     core_ref, factor_ref, table_ref, mask_ref, q00, q01, q10, q11, gain_ref, weight_ref, out_weight_ref,
-    send_ref, keep_ref, d00, d01, d10, d11, gain_out, scale_out, table_out,
+    send_ref, keep_ref, d00, d10, dlon, gain_out, scale_out, table_out,
     grid3, up, tokt, projt, exps, inv, hot, doutt, means,
 ):
     places = ((0, 0), (0, 8), (8, 0), (8, 8))
@@ -174,7 +174,7 @@
         hot[pl.ds(at, HEAD_DIM), :] = mixed[:HEAD_DIM, :] * inverse
         return carry
 
-    lax.fori_loop(0, HEADS, forward_head, 0, unroll=12)
+    lax.fori_loop(0, HEADS, forward_head, 0, unroll=24)
 
     keep_ref[384:768, :] = rows_of(hot, mine)
     send_ref[384:768, :] = rows_of(hot, 1 - mine)
@@ -241,8 +241,11 @@
 
     dtokens = up[...] + mm(weight_ref[...], send_ref[768:3072, :]).T
     grid3[...] = dtokens.reshape(WIN, WIN, D)
-    for (r, c), part in zip(places, (d00, d01, d10, d11)):
-        part[...] = grid3[r : r + 8, c : c + 8, :].reshape(QUAD, D).astype(bf16)
+    pieces = [grid3[r : r + 8, c : c + 8, :].reshape(QUAD, D).astype(bf16) for r, c in places]
+    d00[...] = pieces[0]
+    d10[...] = pieces[2]
+    dlon[0:QUAD, :] = pieces[1]
+    dlon[QUAD:, :] = pieces[3]
 
 
 def table_kernel(outer_ref, hidden_ref, slope_ref, table_ref, gain_ref, scale_ref, pack_ref, rows_ref, work_ref):
@@ -401,7 +404,7 @@
         in_specs=[HBM] * 2,
         out_specs=tuple(vmem(4)),
         scratch_shapes=[pltpu.VMEM((WIN, WIN, D), bf16)] * 2 + [pltpu.SemaphoreType.DMA((2,))],
-        compiler_params=params(16),
+        compiler_params=params(60),
         cost_estimate=cost(2),
         name="cut",
     )(features, upstream)
@@ -433,21 +436,20 @@
     )(last, logit_scale, table_inner, offset_row, outer_t, validity, norm_gain)
 
     quad_shape = jax.ShapeDtypeStruct((QUAD, D), bf16)
-    send, keep, *dquads, gain_part, scale_part, table_part = pl.pallas_call(
+    send, keep, d00, d10, dlon, gain_part, scale_part, table_part = pl.pallas_call(
         window_kernel,
         out_shape=(
             jax.ShapeDtypeStruct((3840, AREA), bf16),
             jax.ShapeDtypeStruct((768, AREA), bf16),
             quad_shape,
             quad_shape,
-            quad_shape,
-            quad_shape,
+            jax.ShapeDtypeStruct((2 * QUAD, D), bf16),
             jax.ShapeDtypeStruct((1, D), f32),
             jax.ShapeDtypeStruct((HEADS, AREA), f32),
             jax.ShapeDtypeStruct((HEADS, WIN, 512), f32),
         ),
         in_specs=[SMEM] + vmem(10),
-        out_specs=tuple(vmem(9)),
+        out_specs=tuple(vmem(8)),
         scratch_shapes=[
             pltpu.VMEM((WIN, WIN, D), f32),
             pltpu.VMEM((AREA, D), f32),
@@ -476,6 +478,8 @@
         name="table",
     )(outer_t, hidden, slope, table_part, gain_part, scale_part)
     got_pack = lax.ppermute(pack, BOTH, CORES)
+    from_lon = lax.ppermute(dlon, BOTH, shift_pairs(0, 1))
+    got_pack, from_lon = lax.optimization_barrier((got_pack, from_lon))
     grads = pl.pallas_call(
         grads_kernel,
         out_shape=jax.ShapeDtypeStruct((16, 200, PART), bf16),
@@ -494,14 +498,9 @@
         cost_estimate=cost(1),
         name="plane",
     )(exchange(grads, PLANE))
-    late = lax.optimization_barrier((plane, *dquads))
-    plane, dquads = late[0], late[1:]
-    back = [
-        value if step == (0, 0) else lax.ppermute(value, BOTH, shift_pairs(*step))
-        for step, value in zip(steps, dquads)
-    ]
-    held = lax.optimization_barrier((exchange(plane, COLUMN), *back))
-    column, back = held[0], held[1:]
+    plane, d10, from_lon = lax.optimization_barrier((plane, d10, from_lon))
+    from_lat = lax.ppermute(jnp.concatenate([d10, from_lon[QUAD:]], 0), BOTH, shift_pairs(1, 0))
+    column, from_lat = lax.optimization_barrier((exchange(plane, COLUMN), from_lat))
     column = pl.pallas_call(
         column_kernel,
         out_shape=jax.ShapeDtypeStruct((8, 32, PART), bf16),
@@ -512,7 +511,7 @@
         name="column",
     )(column)
 
-    back = [value.reshape(SHIFT, SHIFT, D) for value in back]
+    back = [value.reshape(SHIFT, SHIFT, D) for value in (d00, from_lon[:QUAD], from_lat[:QUAD], from_lat[QUAD:])]
     input_delta = jnp.concatenate(
         [jnp.concatenate([back[3], back[2]], 1), jnp.concatenate([back[1], back[0]], 1)], 0
     )

time: 110 us -> 109 us (level)
  waiting for transfers between devices: 11.4 us -> 16.9 us
  blocking collectives: 47.9 us -> 43.9 us
  local copies, waits for them, and re-layouts: 2.02 us -> 0.07 us
  starting transfers between devices: 20.1 us -> 18.3 us
  Pallas kernels: 27 us -> 28.1 us
    all_to_all x2, blocking collectives: 47.9 us -> 43.9 us  [exchange(): lax.all_to_all(value, BOTH, 0, 0, axis_index_groups=groups, tiled=True)]
    all_to_all x1, waiting for transfers between devices: 1.5 us -> 3.99 us  [exchange(): lax.all_to_all(value, BOTH, 0, 0, axis_index_groups=groups, tiled=True)]
    ppermute x3 -> x2, waiting for transfers between devices: 7.15 us -> 9.64 us  [the longest x1 5.34 us: per_device(): lax.ppermute(jnp.concatenate([d10, from_lon[QUAD:]], 0), BOTH, shift_pair...]
    unnamed x20 -> x18, local copies, waits for them, and re-layouts: 2.02 us -> 0.04 us
    pallas_call x1, Pallas kernels: 0.45 us -> 2.05 us  [per_device(): pl.pallas_call(cut_kernel, out_shape=(jax.ShapeDtypeStruct((2 * QUAD, D),...]
    ppermute x3 -> x2, starting transfers between devices: 2.24 us -> 0.9 us  [the longest x1 0.5 us: per_device(): from_lon = lax.ppermute(dlon, BOTH, shift_pairs(0, 1))]
  transfers between devices with their start and end apart: 9 -> 8, of which waited for: 6 -> 6; matrix products, arithmetic and copies ran while one was open for 0% -> 0% of each run, Pallas kernels for 6% -> 6%
where the time goes in v3:
time: 109 us
  blocking collectives  43.9 us (40%)
  Pallas kernels  28.1 us (26%)
  starting transfers between devices  18.3 us (17%)
  waiting for transfers between devices  16.9 us (16%)
    all_to_all x2, blocking collectives, exchange(): lax.all_to_all(value, BOTH, 0, 0, axis_index_groups=groups, tiled=True)  43.9 us
    pallas_call x1, Pallas kernels, per_device(): pl.pallas_call(window_kernel, out_shape=(jax.ShapeDtypeStruct((3840, AREA...  15.1 us
    ppermute x3, starting transfers between devices, per_device(): lax.ppermute(value, BOTH, shift_pairs(-step[0], -step[1]))  10.3 us
    all_to_all x1, starting transfers between devices, exchange(): lax.all_to_all(value, BOTH, 0, 0, axis_index_groups=groups, tiled=True)  6.86 us
    ppermute x1, waiting for transfers between devices, per_device(): lax.ppermute(jnp.concatenate([d10, from_lon[QUAD:]], 0), BOTH, shift_pair...  5.34 us
    ppermute x1, waiting for transfers between devices, per_device(): from_lon = lax.ppermute(dlon, BOTH, shift_pairs(0, 1))  4.3 us
    all_to_all x1, waiting for transfers between devices, exchange(): lax.all_to_all(value, BOTH, 0, 0, axis_index_groups=groups, tiled=True)  3.99 us
    pallas_call x1, Pallas kernels, per_device(): pl.pallas_call(table_kernel, out_shape=jax.ShapeDtypeStruct((64, PART), b...  3.76 us
  transfers between devices with their start and end apart: 8, of which 6 were waited for; matrix products, arithmetic and copies ran while one was open for 0% of the time, Pallas kernels for 6%

profile of v3, /device:TPU:2, one launch (start us, length us, event | category | flops | bytes accessed | tf_op | source)
XLA Modules:
  0.0 108.9 jit_solution(5586262887160461434)
XLA Ops:
  0.6 0.0 copy-start.3
  0.6 0.0 copy-start.2
  0.7 0.0 copy-start.6
  0.7 0.0 copy-start.4
  0.7 0.0 copy-start.7
  0.7 0.0 copy-start.5
  0.7 2.1 %cut.1 = (bf16[128,768]{1,0:T(8,128)(2,1)}, bf16[128,768]{1,0:T(8,128)(2,1)}, bf16[128,768]{1,0:T(8,128)(2,1)}, bf16[128,768]{1,0:T(8,128)(2,1)}) custom-call(bf16[16,16,768]{2,1,0:T(8,128)(2,1)} %features_hbm.1, bf16[16,16,768]{2,1,0:T(8,128)(2,1)} %upstream_hbm.1), custom_call_target="tpu_custom_call" | custom-call | flops 2300000000 | tf_op jit(solution)/shard_map/cut/pallas_call | solution.py:401
  2.8 6.9 %collective-permute-start = (bf16[128,768]{1,0:T(8,128)(2,1)}, bf16[128,768]{1,0:T(8,128)(2,1)S(1)}, u32[]{:S(2)}, u32[]{:S(2)}) collective-permute-start(bf16[128,768]{1,0:T(8,128)(2,1)} %get-tuple-element.46), channel_id=1, source_target_pairs={{0,31},{1,0},{2,1},{3,2},{4,3},{5,4},{6,5},{7,6},{8,7},{9,8},{10,9... | collective-permute-start | bytes 589832 | tf_op jit(solution)/shard_map/ppermute | solution.py:412
  9.7 1.4 %collective-permute-start.1 = (bf16[128,768]{1,0:T(8,128)(2,1)}, bf16[128,768]{1,0:T(8,128)(2,1)S(1)}, u32[]{:S(2)}, u32[]{:S(2)}) collective-permute-start(bf16[128,768]{1,0:T(8,128)(2,1)} %get-tuple-element.47), channel_id=1, source_target_pairs={{0,224},{1,225},{2,226},{3,227},{4,228},{5,229},{6,230},{7,231},{8... | collective-permute-start | bytes 589832 | tf_op jit(solution)/shard_map/ppermute | solution.py:412
  11.1 2.0 %collective-permute-start.2 = (bf16[128,768]{1,0:T(8,128)(2,1)}, bf16[128,768]{1,0:T(8,128)(2,1)S(1)}, u32[]{:S(2)}, u32[]{:S(2)}) collective-permute-start(bf16[128,768]{1,0:T(8,128)(2,1)} %get-tuple-element.48), channel_id=1, source_target_pairs={{0,255},{1,224},{2,225},{3,226},{4,227},{5,228},{6,229},{7,230},{8... | collective-permute-start | bytes 589832 | tf_op jit(solution)/shard_map/ppermute | solution.py:412
  13.1 0.0 copy-done.3
  13.1 0.0 copy-done.2
  13.1 0.0 copy-done.6
  13.1 0.0 copy-done.4
  13.1 0.0 copy-done.7
  13.1 0.0 copy-done.5
  13.1 0.0 copy-start
  13.1 0.0 copy-start.1
  13.2 0.0 copy-start.8
  13.2 3.3 %bias.1 = (f32[24,16,512]{2,1,0:T(8,128)S(1)}, f32[256,256]{1,0:T(8,128)S(1)}, f32[24,1,256]{2,1,0:T(1,128)S(1)}, f32[1024,512]{1,0:T(8,128)S(1)}, f32[24,1024]{1,0:T(8,128)S(1)}, /*index=5*/f32[1,768]{1,0:T(1,128)S(1)}) custom-call(s32[1]{0:T(128)} %bitcast.1.last_ref, f32[24]{0:T(128)S(1)} %copy-done.7, f32[2,512]{1,0:T(2,128)S(1)} %copy-done.4, ...), custom_call_target="tpu_custom_call" | custom-call | flops 2300000000 | tf_op jit(solution)/shard_map/bias/pallas_call | solution.py:420
  16.5 0.0 collective-permute-done.q01
  16.5 1.2 %collective-permute-done.1.q10 = bf16[128,768]{1,0:T(8,128)(2,1)S(1)} collective-permute-done((bf16[128,768]{1,0:T(8,128)(2,1)}, bf16[128,768]{1,0:T(8,128)(2,1)S(1)}, u32[]{:S(2)}, u32[]{:S(2)}) %collective-permute-start.1) | collective-permute-done | bytes 196640 | tf_op jit(solution)/shard_map/ppermute | solution.py:412
  17.7 0.8 collective-permute-done.2.q11
  18.6 0.0 copy-done
  18.6 0.0 copy-done.1
  18.6 0.0 copy-done.8
  18.6 15.1 %window.1 = (bf16[3840,256]{1,0:T(8,128)(2,1)S(1)}, bf16[768,256]{1,0:T(8,128)(2,1)S(1)}, bf16[64,768]{1,0:T(8,128)(2,1)S(1)}, bf16[64,768]{1,0:T(8,128)(2,1)S(1...) custom-call(s32[1]{0:T(128)} %bitcast.core_ref, ...), custom_call_target="tpu_custom_call" | custom-call | flops 19549999104 | tf_op jit(solution)/shard_map/window/pallas_call | solution.py:439
  33.7 0.1 collective-permute-start.3
  33.8 0.5 collective-permute-start.5
  34.3 3.8 %table.1.pack_ref = bf16[64,384]{1,0:T(8,128)(2,1)S(1)} custom-call(f32[24,512]{1,0:T(8,128)S(1)} %bitcast.14, f32[1024,512]{1,0:T(8,128)S(1)} %get-tuple-element.52.hidden_ref, f32[24,1024]{1,0:T(8,128)S(1)} %get-tuple-element.53.slope_ref, f32[24,16,512]{2,1,0:T(8,128)S(1)} %get-tuple-element.54.table_ref, f32[1,768]{1,0:T(1,128)S(1)} %get-tuple-element.55.gain_ref, ...), custom_call_target="tpu_custom_call" | custom-call | flops 5750000128 | tf_op jit(solution)/shard_map/table/pallas_call | solution.py:470
  38.1 0.1 collective-permute-start.4
  38.2 1.2 %collective-permute-done.4.got_pack_ref = bf16[64,384]{1,0:T(8,128)(2,1)S(1)} collective-permute-done((bf16[64,384]{1,0:T(8,128)(2,1)S(1)}, bf16[64,384]{1,0:T(8,128)(2,1)S(1)}, u32[]{:S(2)}, u32[]{:S(2)}) %collective-permute-start.4) | collective-permute-done | bytes 49184 | tf_op jit(solution)/shard_map/ppermute | solution.py:480
  39.4 4.3 %collective-permute-done.5 = bf16[128,768]{1,0:T(8,128)(2,1)S(1)} collective-permute-done((bf16[128,768]{1,0:T(8,128)(2,1)S(1)}, bf16[128,768]{1,0:T(8,128)(2,1)S(1)}, u32[]{:S(2)}, u32[]{:S(2)}) %collective-permute-start.5) | collective-permute-done | bytes 196640 | tf_op jit(solution)/shard_map/ppermute | solution.py:481
  43.7 0.0 collective-permute-done.3.got_ref
  43.7 2.1 %grads.1 = bf16[16,200,384]{2,1,0:T(8,128)(2,1)S(1)} custom-call(bf16[768,256]{1,0:T(8,128)(2,1)S(1)} %get-tuple-element.50.keep_ref, bf16[3840,256]{1,0:T(8,128)(2,1)S(1)} %get-tuple-element.51.send_ref, bf16[3840,256]{1,0:T(8,128)(2,1)S(1)} %collective-permute-done.3.got_ref, bf16[64,384]{1,0:T(8,128)(2,1)S(1)} %table.1.pack_ref, ...), custom_call_target="tpu_custom_call" | custom-call | flops 2300000000 | tf_op jit(solution)/shard_map/grads/pallas_call | solution.py:483
  45.8 34.3 %all_to_all.15.in_ref = bf16[16,200,384]{2,1,0:T(8,128)(2,1)S(1)} all-to-all(bf16[16,200,384]{2,1,0:T(8,128)(2,1)S(1)} %grads.1), channel_id=1, replica_groups={{0,32,64,96,128,160,192,224,16,48,80,112,144,176,208,240},{1,33,65,97,1..., dimensions={0} | all-to-all | bytes 4915200 | tf_op jit(solution)/shard_map/all_to_all | solution.py:393
  80.1 1.0 plane.1
  81.1 6.9 %all-to-all-start.1 = ((bf16[8,32,384]{2,1,0:T(8,128)(2,1)}), bf16[8,32,384]{2,1,0:T(8,128)(2,1)S(1)}, u32[]{:S(2)}, u32[]{:S(2)}) async-start(bf16[8,32,384]{2,1,0:T(8,128)(2,1)} %plane.1), calls=%async_computation.1 | async-start | bytes 393216 | tf_op jit(solution)/shard_map/all_to_all | solution.py:393
  88.0 0.4 collective-permute-start.6
  88.4 5.3 %collective-permute-done.6 = bf16[128,768]{1,0:T(8,128)(2,1)S(1)} collective-permute-done((bf16[128,768]{1,0:T(8,128)(2,1)S(1)}, bf16[128,768]{1,0:T(8,128)(2,1)S(1)}, u32[]{:S(2)}, u32[]{:S(2)}) %collective-permute-start.6) | collective-permute-done | bytes 196640 | tf_op jit(solution)/shard_map/ppermute | solution.py:502
  93.7 4.0 %all-to-all-done.1.in_ref = bf16[8,32,384]{2,1,0:T(8,128)(2,1)S(1)} async-done(((bf16[8,32,384]{2,1,0:T(8,128)(2,1)}), bf16[8,32,384]{2,1,0:T(8,128)(2,1)S(1)}, u32[]{:S(2)}, u32[]{:S(2)}) %all-to-all-start.1) | async-done | bytes 196640 | tf_op jit(solution)/shard_map/all_to_all | solution.py:393
  97.8 0.8 maximum_maximum_fusion
  98.6 9.6 %all_to_all.16.in_ref = bf16[8,32,384]{2,1,0:T(8,128)(2,1)S(1)} all-to-all(bf16[8,32,384]{2,1,0:T(8,128)(2,1)S(1)} %column.1), channel_id=1, replica_groups={{0,32,64,96,128,160,192,224},{1,33,65,97,129,161,193,225},{2,34,66,98,1..., dimensions={0} | all-to-all | bytes 393216 | tf_op jit(solution)/shard_map/all_to_all | solution.py:393
  108.1 0.7 finish.1
  (4 shorter events, 0.1 us)
Async XLA Ops:
  0.6 12.5 %copy-start.3 = (s32[16,16]{1,0:T(8,128)S(1)}, s32[16,16]{1,0:T(8,128)}, u32[]{:S(2)}) copy-start(s32[16,16]{1,0:T(8,128)} %valid_ref.1) | copy-start | bytes 3076
  0.6 12.5 %copy-start.2 = (f32[512,24]{0,1:T(8,128)S(1)}, f32[512,24]{0,1:T(8,128)}, u32[]{:S(2)}) copy-start(f32[512,24]{0,1:T(8,128)} %param.18) | copy-start | bytes 147460
  0.7 12.5 %copy-start.6 = (f32[512]{0:T(512)S(1)}, f32[512]{0:T(512)}, u32[]{:S(2)}) copy-start(f32[512]{0:T(512)} %param.17) | copy-start | bytes 6148
  0.7 12.4 %copy-start.4 = (f32[2,512]{1,0:T(2,128)S(1)}, f32[2,512]{1,0:T(2,128)}, u32[]{:S(2)}) copy-start(f32[2,512]{1,0:T(2,128)} %inner_ref.1) | copy-start | bytes 12292
  0.7 12.4 %copy-start.7 = (f32[24]{0:T(128)S(1)}, f32[24]{0:T(128)}, u32[]{:S(2)}) copy-start(f32[24]{0:T(128)} %log_ref.1) | copy-start | bytes 292
  0.7 12.4 %copy-start.5 = (f32[768]{0:T(1024)S(1)}, f32[768]{0:T(1024)}, u32[]{:S(2)}) copy-start(f32[768]{0:T(1024)} %gain_ref.1) | copy-start | bytes 9220
  2.8 13.7 %collective-permute-start = (bf16[128,768]{1,0:T(8,128)(2,1)}, bf16[128,768]{1,0:T(8,128)(2,1)S(1)}, u32[]{:S(2)}, u32[]{:S(2)}) collective-permute-start(bf16[128,768]{1,0:T(8,128)(2,1)} %get-tuple-element.46), channel_id=1, source_target_pairs={{0,31},{1,0},{2,1},{3,2},{4,3},{5,4},{6,5},{7,6},{8,7},{9,8},{10,9... | collective-permute-start | bytes 589832 | tf_op jit(solution)/shard_map/ppermute | solution.py:412
  9.7 8.0 %collective-permute-start.1 = (bf16[128,768]{1,0:T(8,128)(2,1)}, bf16[128,768]{1,0:T(8,128)(2,1)S(1)}, u32[]{:S(2)}, u32[]{:S(2)}) collective-permute-start(bf16[128,768]{1,0:T(8,128)(2,1)} %get-tuple-element.47), channel_id=1, source_target_pairs={{0,224},{1,225},{2,226},{3,227},{4,228},{5,229},{6,230},{7,231},{8... | collective-permute-start | bytes 589832 | tf_op jit(solution)/shard_map/ppermute | solution.py:412
  11.1 7.5 %collective-permute-start.2 = (bf16[128,768]{1,0:T(8,128)(2,1)}, bf16[128,768]{1,0:T(8,128)(2,1)S(1)}, u32[]{:S(2)}, u32[]{:S(2)}) collective-permute-start(bf16[128,768]{1,0:T(8,128)(2,1)} %get-tuple-element.48), channel_id=1, source_target_pairs={{0,255},{1,224},{2,225},{3,226},{4,227},{5,228},{6,229},{7,230},{8... | collective-permute-start | bytes 589832 | tf_op jit(solution)/shard_map/ppermute | solution.py:412
  13.1 5.4 %copy-start = (bf16[768,2304]{1,0:T(8,128)(2,1)S(1)}, bf16[768,2304]{1,0:T(8,128)(2,1)}, u32[]{:S(2)}) copy-start(bf16[768,2304]{1,0:T(8,128)(2,1)} %weight_ref.1) | copy-start | bytes 10616836
  13.1 5.4 %copy-start.1 = (bf16[768,768]{1,0:T(8,128)(2,1)S(1)}, bf16[768,768]{1,0:T(8,128)(2,1)}, u32[]{:S(2)}) copy-start(bf16[768,768]{1,0:T(8,128)(2,1)} %out_weight_ref.1) | copy-start | bytes 3538948
  13.2 5.4 %copy-start.8 = (bf16[128,768]{1,0:T(8,128)(2,1)S(1)}, bf16[128,768]{1,0:T(8,128)(2,1)}, u32[]{:S(2)}) copy-start(bf16[128,768]{1,0:T(8,128)(2,1)} %get-tuple-element.45.q00) | copy-start | bytes 589828
  33.7 10.0 %collective-permute-start.3 = (bf16[3840,256]{1,0:T(8,128)(2,1)S(1)}, bf16[3840,256]{1,0:T(8,128)(2,1)S(1)}, u32[]{:S(2)}, u32[]{:S(2)}) collective-permute-start(bf16[3840,256]{1,0:T(8,128)(2,1)S(1)} %get-tuple-element.51.send_ref), channel_id=1, source_target_pairs={{0,1},{1,0},{2,3},{3,2},{4,5},{5,4},{6,7},{7,6},{8,9},{9,8},{10,11... | collective-permute-start | bytes 5898248 | tf_op jit(solution)/shard_map/ppermute | solution.py:469
  33.8 9.9 %collective-permute-start.5 = (bf16[128,768]{1,0:T(8,128)(2,1)S(1)}, bf16[128,768]{1,0:T(8,128)(2,1)S(1)}, u32[]{:S(2)}, u32[]{:S(2)}) collective-permute-start(bf16[128,768]{1,0:T(8,128)(2,1)S(1)} %get-tuple-element.57), channel_id=1, source_target_pairs={{0,1},{1,2},{2,3},{3,4},{4,5},{5,6},{6,7},{7,8},{8,9},{9,10},{10,1... | collective-permute-start | bytes 589832 | tf_op jit(solution)/shard_map/ppermute | solution.py:481
  38.1 1.3 %collective-permute-start.4 = (bf16[64,384]{1,0:T(8,128)(2,1)S(1)}, bf16[64,384]{1,0:T(8,128)(2,1)S(1)}, u32[]{:S(2)}, u32[]{:S(2)}) collective-permute-start(bf16[64,384]{1,0:T(8,128)(2,1)S(1)} %table.1.pack_ref), channel_id=1, source_target_pairs={{0,1},{1,0},{2,3},{3,2},{4,5},{5,4},{6,7},{7,6},{8,9},{9,8},{10,11... | collective-permute-start | bytes 147464 | tf_op jit(solution)/shard_map/ppermute | solution.py:480
  81.1 16.6 %all-to-all-start.1 = ((bf16[8,32,384]{2,1,0:T(8,128)(2,1)}), bf16[8,32,384]{2,1,0:T(8,128)(2,1)S(1)}, u32[]{:S(2)}, u32[]{:S(2)}) async-start(bf16[8,32,384]{2,1,0:T(8,128)(2,1)} %plane.1), calls=%async_computation.1 | async-start | bytes 393216 | tf_op jit(solution)/shard_map/all_to_all | solution.py:393
  88.0 5.7 %collective-permute-start.6 = (bf16[128,768]{1,0:T(8,128)(2,1)S(1)}, bf16[128,768]{1,0:T(8,128)(2,1)S(1)}, u32[]{:S(2)}, u32[]{:S(2)}) collective-permute-start(bf16[128,768]{1,0:T(8,128)(2,1)S(1)} %pad_maximum_fusion), channel_id=1, source_target_pairs={{0,32},{1,33},{2,34},{3,35},{4,36},{5,37},{6,38},{7,39},{8,40},{9,... | collective-permute-start | bytes 589832 | tf_op jit(solution)/shard_map/ppermute | solution.py:502

commit v4 on v3

--- a/solution.py
+++ b/solution.py
@@ -73,11 +73,13 @@
 
 def bias_kernel(
     last_ref, log_ref, inner_ref, offset_ref, outer_ref, valid_ref, gain_ref,
-    table_ref, mask_ref, factor_ref, hidden_ref, slope_ref, gain_out, rows_ref,
+    table_ref, mask_ref, factor_ref, high_ref, low_ref, slope_ref, gain_out, rows_ref,
 ):
     gain_out[...] = gain_ref[...].reshape(1, D)
     hidden = hidden_of(inner_ref, offset_ref)
-    hidden_ref[...] = hidden
+    high = hidden.astype(bf16)
+    high_ref[...] = high
+    low_ref[...] = (hidden - high.astype(f32)).astype(bf16)
     sig = jax.nn.sigmoid(mm(outer_ref[...], hidden, NT, exact))
     grid = 16.0 * sig
     slope_ref[...] = grid * (1.0 - sig)
@@ -248,9 +250,10 @@
     dlon[QUAD:, :] = pieces[3]
 
 
-def table_kernel(outer_ref, hidden_ref, slope_ref, table_ref, gain_ref, scale_ref, pack_ref, rows_ref, work_ref):
+def table_kernel(
+    outer_ref, high_ref, low_ref, slope_ref, table_ref, gain_ref, scale_ref, pack_ref, rows_ref, work_ref
+):
     first_coord, second_coord = slot_coords()
-    hidden = hidden_ref[...]
     lane = lax.broadcasted_iota(jnp.int32, (HEADS, 512), 1)
     first = (lane % 32) < 16
     for head in range(HEADS):
@@ -263,9 +266,18 @@
         odd = odd + pltpu.roll(jnp.where(first, 0.0, row), (512 - 1 - cj) % 512, 1)
     dgrid = jnp.concatenate([even, odd], 1)
     dlogits = dgrid * slope_ref[...]
-    outer = mm(dlogits, hidden, NN, exact)
-    dhidden = mm(dlogits, outer_ref[...], TN, exact)
-    dhidden = jnp.where(hidden > 0.0, dhidden, 0.0)
+    top = dlogits.astype(bf16).astype(f32)
+    rest = dlogits - top
+    pair = jnp.concatenate([top, rest], 0).astype(bf16)
+    high = high_ref[...]
+    outer = mm(pair, high)
+    outer = outer[:HEADS] + outer[HEADS:] + mm(pair, low_ref[...])[:HEADS]
+    weight = outer_ref[...]
+    weight_top = weight.astype(bf16).astype(f32)
+    zeros = jnp.zeros((8, SLOTS), f32)
+    left = jnp.concatenate([top, rest, top, zeros], 0).astype(bf16)
+    right = jnp.concatenate([weight_top, weight_top, weight - weight_top, zeros[:, :HIDDEN]], 0).astype(bf16)
+    dhidden = jnp.where(high.astype(f32) > 0.0, mm(left, right, TN), 0.0)
     scale = jnp.sum(scale_ref[...], -1, keepdims=True)
     where_row = lax.broadcasted_iota(jnp.int32, (HEADS, PART), 0)
     where_lane = lax.broadcasted_iota(jnp.int32, (HEADS, PART), 1)
@@ -408,27 +420,27 @@
         cost_estimate=cost(2),
         name="cut",
     )(features, upstream)
-    moved = [
-        value if step == (0, 0) else lax.ppermute(value, BOTH, shift_pairs(-step[0], -step[1]))
-        for step, value in zip(steps, both)
-    ]
+    moved = [both[0], None, None, None]
+    for n in (3, 2, 1):
+        moved[n] = lax.ppermute(both[n], BOTH, shift_pairs(-steps[n][0], -steps[n][1]))
 
     outer_t = table_outer.T
     offset_row = table_offset.reshape(1, HIDDEN)
     last = (lax.axis_index("lat") == lax.axis_size("lat") - 1).astype(jnp.int32).reshape(1)
     core = (lax.axis_index("lon") % 2).astype(jnp.int32).reshape(1)
-    bias, mask, factor, hidden, slope, gain_row = pl.pallas_call(
+    bias, mask, factor, hidden_high, hidden_low, slope, gain_row = pl.pallas_call(
         bias_kernel,
         out_shape=(
             jax.ShapeDtypeStruct((HEADS, WIN, 512), f32),
             jax.ShapeDtypeStruct((AREA, AREA), f32),
             jax.ShapeDtypeStruct((HEADS, 1, AREA), f32),
-            jax.ShapeDtypeStruct((SLOTS, HIDDEN), f32),
+            jax.ShapeDtypeStruct((SLOTS, HIDDEN), bf16),
+            jax.ShapeDtypeStruct((SLOTS, HIDDEN), bf16),
             jax.ShapeDtypeStruct((HEADS, SLOTS), f32),
             jax.ShapeDtypeStruct((1, D), f32),
         ),
         in_specs=[SMEM] * 2 + vmem(5),
-        out_specs=tuple(vmem(6)),
+        out_specs=tuple(vmem(7)),
         scratch_shapes=[pltpu.VMEM((WIN, HEADS, 512), f32)],
         compiler_params=params(16),
         cost_estimate=cost(2),
@@ -470,13 +482,13 @@
     pack = pl.pallas_call(
         table_kernel,
         out_shape=jax.ShapeDtypeStruct((64, PART), bf16),
-        in_specs=vmem(6),
+        in_specs=vmem(7),
         out_specs=vmem(1)[0],
         scratch_shapes=[pltpu.VMEM((WIN, HEADS, 512), f32), pltpu.VMEM((64, PART), f32)],
         compiler_params=params(16),
         cost_estimate=cost(5),
         name="table",
-    )(outer_t, hidden, slope, table_part, gain_part, scale_part)
+    )(outer_t, hidden_high, hidden_low, slope, table_part, gain_part, scale_part)
     got_pack = lax.ppermute(pack, BOTH, CORES)
     from_lon = lax.ppermute(dlon, BOTH, shift_pairs(0, 1))
     got_pack, from_lon = lax.optimization_barrier((got_pack, from_lon))

time: 109 us -> 107 us (0.982)
  blocking collectives: 43.9 us -> 41.9 us
  waiting for transfers between devices: 16.9 us -> 18.8 us
  Pallas kernels: 28.1 us -> 26.4 us
    all_to_all x2, blocking collectives: 43.9 us -> 41.9 us  [exchange(): lax.all_to_all(value, BOTH, 0, 0, axis_index_groups=groups, tiled=True)]
    pallas_call x1, Pallas kernels: 3.76 us -> 1.94 us  [per_device(): pl.pallas_call(table_kernel, out_shape=jax.ShapeDtypeStruct((64, PART), b...]
    ppermute x1, waiting for transfers between devices: 4.3 us -> 5.85 us  [per_device(): from_lon = lax.ppermute(dlon, BOTH, shift_pairs(0, 1))]
  transfers between devices with their start and end apart: 8 -> 8, of which waited for: 6 -> 6; matrix products, arithmetic and copies ran while one was open for 0% -> 0% of each run, Pallas kernels for 6% -> 5%
where the time goes in v4:
time: 107 us
  blocking collectives  41.9 us (39%)
  Pallas kernels  26.4 us (25%)
  waiting for transfers between devices  18.8 us (18%)
  starting transfers between devices  18.2 us (17%)
    all_to_all x2, blocking collectives, exchange(): lax.all_to_all(value, BOTH, 0, 0, axis_index_groups=groups, tiled=True)  41.9 us
    pallas_call x1, Pallas kernels, per_device(): pl.pallas_call(window_kernel, out_shape=(jax.ShapeDtypeStruct((3840, AREA...  15.1 us
    ppermute x3, starting transfers between devices, per_device(): lax.ppermute(both[n], BOTH, shift_pairs(-steps[n][0], -steps[n][1]))  10.3 us
    all_to_all x1, starting transfers between devices, exchange(): lax.all_to_all(value, BOTH, 0, 0, axis_index_groups=groups, tiled=True)  7.01 us
    ppermute x1, waiting for transfers between devices, per_device(): from_lon = lax.ppermute(dlon, BOTH, shift_pairs(0, 1))  5.85 us
    ppermute x1, waiting for transfers between devices, per_device(): lax.ppermute(jnp.concatenate([d10, from_lon[QUAD:]], 0), BOTH, shift_pair...  5.55 us
    all_to_all x1, waiting for transfers between devices, exchange(): lax.all_to_all(value, BOTH, 0, 0, axis_index_groups=groups, tiled=True)  3.99 us
    pallas_call x1, Pallas kernels, per_device(): pl.pallas_call(bias_kernel, out_shape=(jax.ShapeDtypeStruct((HEADS, WIN,...  3.52 us
  transfers between devices with their start and end apart: 8, of which 6 were waited for; matrix products, arithmetic and copies ran while one was open for 0% of the time, Pallas kernels for 5%

profile of v4, /device:TPU:2, one launch (start us, length us, event | category | flops | bytes accessed | tf_op | source)
XLA Modules:
  0.0 107.0 jit_solution(1377755608165471084)
XLA Ops:
  0.6 0.0 copy-start.3
  0.6 0.0 copy-start.2
  0.7 0.0 copy-start.6
  0.7 0.0 copy-start.4
  0.7 0.0 copy-start.7
  0.7 0.0 copy-start.5
  0.7 2.1 %cut.1 = (bf16[128,768]{1,0:T(8,128)(2,1)}, bf16[128,768]{1,0:T(8,128)(2,1)}, bf16[128,768]{1,0:T(8,128)(2,1)}, bf16[128,768]{1,0:T(8,128)(2,1)}) custom-call(bf16[16,16,768]{2,1,0:T(8,128)(2,1)} %features_hbm.1, bf16[16,16,768]{2,1,0:T(8,128)(2,1)} %upstream_hbm.1), custom_call_target="tpu_custom_call" | custom-call | flops 2300000000 | tf_op jit(solution)/shard_map/cut/pallas_call | solution.py:413
  2.8 6.9 %collective-permute-start = (bf16[128,768]{1,0:T(8,128)(2,1)}, bf16[128,768]{1,0:T(8,128)(2,1)S(1)}, u32[]{:S(2)}, u32[]{:S(2)}) collective-permute-start(bf16[128,768]{1,0:T(8,128)(2,1)} %get-tuple-element.47), channel_id=1, source_target_pairs={{0,31},{1,0},{2,1},{3,2},{4,3},{5,4},{6,5},{7,6},{8,7},{9,8},{10,9... | collective-permute-start | bytes 589832 | tf_op jit(solution)/shard_map/ppermute | solution.py:425
  9.7 1.4 %collective-permute-start.1 = (bf16[128,768]{1,0:T(8,128)(2,1)}, bf16[128,768]{1,0:T(8,128)(2,1)S(1)}, u32[]{:S(2)}, u32[]{:S(2)}) collective-permute-start(bf16[128,768]{1,0:T(8,128)(2,1)} %get-tuple-element.48), channel_id=1, source_target_pairs={{0,224},{1,225},{2,226},{3,227},{4,228},{5,229},{6,230},{7,231},{8... | collective-permute-start | bytes 589832 | tf_op jit(solution)/shard_map/ppermute | solution.py:425
  11.1 2.0 %collective-permute-start.2 = (bf16[128,768]{1,0:T(8,128)(2,1)}, bf16[128,768]{1,0:T(8,128)(2,1)S(1)}, u32[]{:S(2)}, u32[]{:S(2)}) collective-permute-start(bf16[128,768]{1,0:T(8,128)(2,1)} %get-tuple-element.49), channel_id=1, source_target_pairs={{0,255},{1,224},{2,225},{3,226},{4,227},{5,228},{6,229},{7,230},{8... | collective-permute-start | bytes 589832 | tf_op jit(solution)/shard_map/ppermute | solution.py:425
  13.1 0.0 copy-done.3
  13.1 0.0 copy-done.2
  13.1 0.0 copy-done.6
  13.1 0.0 copy-done.4
  13.1 0.0 copy-done.7
  13.1 0.0 copy-done.5
  13.1 0.0 copy-start
  13.1 0.0 copy-start.1
  13.2 0.0 copy-start.8
  13.2 3.5 %bias.1 = (f32[24,16,512]{2,1,0:T(8,128)S(1)}, f32[256,256]{1,0:T(8,128)S(1)}, f32[24,1,256]{2,1,0:T(1,128)S(1)}, bf16[1024,512]{1,0:T(8,128)(2,1)S(1)}, bf16[10...) custom-call(s32[1]{0:T(128)} %bitcast.1.last_ref, f32[24]{0:T(128)S(1)} %copy-done.7, ...), custom_call_target="tpu_custom_call" | custom-call | flops 2300000000 | tf_op jit(solution)/shard_map/bias/pallas_call | solution.py:431
  16.7 0.0 collective-permute-done.q01
  16.7 1.0 collective-permute-done.1.q10
  17.7 0.8 collective-permute-done.2.q11
  18.6 0.0 copy-done
  18.6 0.0 copy-done.1
  18.6 0.0 copy-done.8
  18.6 15.1 %window.1 = (bf16[3840,256]{1,0:T(8,128)(2,1)S(1)}, bf16[768,256]{1,0:T(8,128)(2,1)S(1)}, bf16[64,768]{1,0:T(8,128)(2,1)S(1)}, bf16[64,768]{1,0:T(8,128)(2,1)S(1...) custom-call(s32[1]{0:T(128)} %bitcast.core_ref, ...), custom_call_target="tpu_custom_call" | custom-call | flops 19549999104 | tf_op jit(solution)/shard_map/window/pallas_call | solution.py:451
  33.7 0.1 collective-permute-start.3
  33.8 0.5 collective-permute-start.5
  34.3 1.9 %table.1.pack_ref = bf16[64,384]{1,0:T(8,128)(2,1)S(1)} custom-call(f32[24,512]{1,0:T(8,128)S(1)} %bitcast.14, bf16[1024,512]{1,0:T(8,128)(2,1)S(1)} %get-tuple-element.53.high_ref, bf16[1024,512]{1,0:T(8,128)(2,1)S(1)} %get-tuple-element.54.low_ref, f32[24,1024]{1,0:T(8,128)S(1)} %get-tuple-element.55.slope_ref, ...), custom_call_target="tpu_custom_call" | custom-call | flops 5750000128 | tf_op jit(solution)/shard_map/table/pallas_call | solution.py:482
  36.2 0.1 collective-permute-start.4
  36.3 1.5 %collective-permute-done.4.got_pack_ref = bf16[64,384]{1,0:T(8,128)(2,1)S(1)} collective-permute-done((bf16[64,384]{1,0:T(8,128)(2,1)S(1)}, bf16[64,384]{1,0:T(8,128)(2,1)S(1)}, u32[]{:S(2)}, u32[]{:S(2)}) %collective-permute-start.4) | collective-permute-done | bytes 49184 | tf_op jit(solution)/shard_map/ppermute | solution.py:492
  37.8 5.8 %collective-permute-done.5 = bf16[128,768]{1,0:T(8,128)(2,1)S(1)} collective-permute-done((bf16[128,768]{1,0:T(8,128)(2,1)S(1)}, bf16[128,768]{1,0:T(8,128)(2,1)S(1)}, u32[]{:S(2)}, u32[]{:S(2)}) %collective-permute-start.5) | collective-permute-done | bytes 196640 | tf_op jit(solution)/shard_map/ppermute | solution.py:493
  43.6 0.0 collective-permute-done.3.got_ref
  43.6 2.1 %grads.1 = bf16[16,200,384]{2,1,0:T(8,128)(2,1)S(1)} custom-call(bf16[768,256]{1,0:T(8,128)(2,1)S(1)} %get-tuple-element.51.keep_ref, bf16[3840,256]{1,0:T(8,128)(2,1)S(1)} %get-tuple-element.52.send_ref, bf16[3840,256]{1,0:T(8,128)(2,1)S(1)} %collective-permute-done.3.got_ref, bf16[64,384]{1,0:T(8,128)(2,1)S(1)} %table.1.pack_ref, ...), custom_call_target="tpu_custom_call" | custom-call | flops 2300000000 | tf_op jit(solution)/shard_map/grads/pallas_call | solution.py:495
  45.7 32.5 %all_to_all.15.in_ref = bf16[16,200,384]{2,1,0:T(8,128)(2,1)S(1)} all-to-all(bf16[16,200,384]{2,1,0:T(8,128)(2,1)S(1)} %grads.1), channel_id=1, replica_groups={{0,32,64,96,128,160,192,224,16,48,80,112,144,176,208,240},{1,33,65,97,1..., dimensions={0} | all-to-all | bytes 4915200 | tf_op jit(solution)/shard_map/all_to_all | solution.py:405
  78.2 1.0 plane.1
  79.2 7.0 %all-to-all-start.1 = ((bf16[8,32,384]{2,1,0:T(8,128)(2,1)}), bf16[8,32,384]{2,1,0:T(8,128)(2,1)S(1)}, u32[]{:S(2)}, u32[]{:S(2)}) async-start(bf16[8,32,384]{2,1,0:T(8,128)(2,1)} %plane.1), calls=%async_computation.1 | async-start | bytes 393216 | tf_op jit(solution)/shard_map/all_to_all | solution.py:405
  86.3 0.2 collective-permute-start.6
  86.5 5.6 %collective-permute-done.6 = bf16[128,768]{1,0:T(8,128)(2,1)S(1)} collective-permute-done((bf16[128,768]{1,0:T(8,128)(2,1)S(1)}, bf16[128,768]{1,0:T(8,128)(2,1)S(1)}, u32[]{:S(2)}, u32[]{:S(2)}) %collective-permute-start.6) | collective-permute-done | bytes 196640 | tf_op jit(solution)/shard_map/ppermute | solution.py:514
  92.0 4.0 %all-to-all-done.1.in_ref = bf16[8,32,384]{2,1,0:T(8,128)(2,1)S(1)} async-done(((bf16[8,32,384]{2,1,0:T(8,128)(2,1)}), bf16[8,32,384]{2,1,0:T(8,128)(2,1)S(1)}, u32[]{:S(2)}, u32[]{:S(2)}) %all-to-all-start.1) | async-done | bytes 196640 | tf_op jit(solution)/shard_map/all_to_all | solution.py:405
  96.1 0.8 maximum_maximum_fusion
  96.8 9.4 %all_to_all.16.in_ref = bf16[8,32,384]{2,1,0:T(8,128)(2,1)S(1)} all-to-all(bf16[8,32,384]{2,1,0:T(8,128)(2,1)S(1)} %column.1), channel_id=1, replica_groups={{0,32,64,96,128,160,192,224},{1,33,65,97,129,161,193,225},{2,34,66,98,1..., dimensions={0} | all-to-all | bytes 393216 | tf_op jit(solution)/shard_map/all_to_all | solution.py:405
  106.3 0.7 finish.1
  (4 shorter events, 0.1 us)
Async XLA Ops:
  0.6 12.5 %copy-start.3 = (s32[16,16]{1,0:T(8,128)S(1)}, s32[16,16]{1,0:T(8,128)}, u32[]{:S(2)}) copy-start(s32[16,16]{1,0:T(8,128)} %valid_ref.1) | copy-start | bytes 3076
  0.6 12.5 %copy-start.2 = (f32[512,24]{0,1:T(8,128)S(1)}, f32[512,24]{0,1:T(8,128)}, u32[]{:S(2)}) copy-start(f32[512,24]{0,1:T(8,128)} %param.18) | copy-start | bytes 147460
  0.7 12.5 %copy-start.6 = (f32[512]{0:T(512)S(1)}, f32[512]{0:T(512)}, u32[]{:S(2)}) copy-start(f32[512]{0:T(512)} %param.17) | copy-start | bytes 6148
  0.7 12.4 %copy-start.4 = (f32[2,512]{1,0:T(2,128)S(1)}, f32[2,512]{1,0:T(2,128)}, u32[]{:S(2)}) copy-start(f32[2,512]{1,0:T(2,128)} %inner_ref.1) | copy-start | bytes 12292
  0.7 12.4 %copy-start.7 = (f32[24]{0:T(128)S(1)}, f32[24]{0:T(128)}, u32[]{:S(2)}) copy-start(f32[24]{0:T(128)} %log_ref.1) | copy-start | bytes 292
  0.7 12.4 %copy-start.5 = (f32[768]{0:T(1024)S(1)}, f32[768]{0:T(1024)}, u32[]{:S(2)}) copy-start(f32[768]{0:T(1024)} %gain_ref.1) | copy-start | bytes 9220
  2.8 13.9 %collective-permute-start = (bf16[128,768]{1,0:T(8,128)(2,1)}, bf16[128,768]{1,0:T(8,128)(2,1)S(1)}, u32[]{:S(2)}, u32[]{:S(2)}) collective-permute-start(bf16[128,768]{1,0:T(8,128)(2,1)} %get-tuple-element.47), channel_id=1, source_target_pairs={{0,31},{1,0},{2,1},{3,2},{4,3},{5,4},{6,5},{7,6},{8,7},{9,8},{10,9... | collective-permute-start | bytes 589832 | tf_op jit(solution)/shard_map/ppermute | solution.py:425
  9.7 8.0 %collective-permute-start.1 = (bf16[128,768]{1,0:T(8,128)(2,1)}, bf16[128,768]{1,0:T(8,128)(2,1)S(1)}, u32[]{:S(2)}, u32[]{:S(2)}) collective-permute-start(bf16[128,768]{1,0:T(8,128)(2,1)} %get-tuple-element.48), channel_id=1, source_target_pairs={{0,224},{1,225},{2,226},{3,227},{4,228},{5,229},{6,230},{7,231},{8... | collective-permute-start | bytes 589832 | tf_op jit(solution)/shard_map/ppermute | solution.py:425
  11.1 7.5 %collective-permute-start.2 = (bf16[128,768]{1,0:T(8,128)(2,1)}, bf16[128,768]{1,0:T(8,128)(2,1)S(1)}, u32[]{:S(2)}, u32[]{:S(2)}) collective-permute-start(bf16[128,768]{1,0:T(8,128)(2,1)} %get-tuple-element.49), channel_id=1, source_target_pairs={{0,255},{1,224},{2,225},{3,226},{4,227},{5,228},{6,229},{7,230},{8... | collective-permute-start | bytes 589832 | tf_op jit(solution)/shard_map/ppermute | solution.py:425
  13.1 5.4 %copy-start = (bf16[768,2304]{1,0:T(8,128)(2,1)S(1)}, bf16[768,2304]{1,0:T(8,128)(2,1)}, u32[]{:S(2)}) copy-start(bf16[768,2304]{1,0:T(8,128)(2,1)} %weight_ref.1) | copy-start | bytes 10616836
  13.1 5.4 %copy-start.1 = (bf16[768,768]{1,0:T(8,128)(2,1)S(1)}, bf16[768,768]{1,0:T(8,128)(2,1)}, u32[]{:S(2)}) copy-start(bf16[768,768]{1,0:T(8,128)(2,1)} %out_weight_ref.1) | copy-start | bytes 3538948
  13.2 5.4 %copy-start.8 = (bf16[128,768]{1,0:T(8,128)(2,1)S(1)}, bf16[128,768]{1,0:T(8,128)(2,1)}, u32[]{:S(2)}) copy-start(bf16[128,768]{1,0:T(8,128)(2,1)} %get-tuple-element.46.q00) | copy-start | bytes 589828
  33.7 10.0 %collective-permute-start.3 = (bf16[3840,256]{1,0:T(8,128)(2,1)S(1)}, bf16[3840,256]{1,0:T(8,128)(2,1)S(1)}, u32[]{:S(2)}, u32[]{:S(2)}) collective-permute-start(bf16[3840,256]{1,0:T(8,128)(2,1)S(1)} %get-tuple-element.52.send_ref), channel_id=1, source_target_pairs={{0,1},{1,0},{2,3},{3,2},{4,5},{5,4},{6,7},{7,6},{8,9},{9,8},{10,11... | collective-permute-start | bytes 5898248 | tf_op jit(solution)/shard_map/ppermute | solution.py:481
  33.8 9.9 %collective-permute-start.5 = (bf16[128,768]{1,0:T(8,128)(2,1)S(1)}, bf16[128,768]{1,0:T(8,128)(2,1)S(1)}, u32[]{:S(2)}, u32[]{:S(2)}) collective-permute-start(bf16[128,768]{1,0:T(8,128)(2,1)S(1)} %get-tuple-element.59), channel_id=1, source_target_pairs={{0,1},{1,2},{2,3},{3,4},{4,5},{5,6},{6,7},{7,8},{8,9},{9,10},{10,1... | collective-permute-start | bytes 589832 | tf_op jit(solution)/shard_map/ppermute | solution.py:493
  36.2 1.6 %collective-permute-start.4 = (bf16[64,384]{1,0:T(8,128)(2,1)S(1)}, bf16[64,384]{1,0:T(8,128)(2,1)S(1)}, u32[]{:S(2)}, u32[]{:S(2)}) collective-permute-start(bf16[64,384]{1,0:T(8,128)(2,1)S(1)} %table.1.pack_ref), channel_id=1, source_target_pairs={{0,1},{1,0},{2,3},{3,2},{4,5},{5,4},{6,7},{7,6},{8,9},{9,8},{10,11... | collective-permute-start | bytes 147464 | tf_op jit(solution)/shard_map/ppermute | solution.py:492
  79.2 16.8 %all-to-all-start.1 = ((bf16[8,32,384]{2,1,0:T(8,128)(2,1)}), bf16[8,32,384]{2,1,0:T(8,128)(2,1)S(1)}, u32[]{:S(2)}, u32[]{:S(2)}) async-start(bf16[8,32,384]{2,1,0:T(8,128)(2,1)} %plane.1), calls=%async_computation.1 | async-start | bytes 393216 | tf_op jit(solution)/shard_map/all_to_all | solution.py:405
  86.3 5.7 %collective-permute-start.6 = (bf16[128,768]{1,0:T(8,128)(2,1)S(1)}, bf16[128,768]{1,0:T(8,128)(2,1)S(1)}, u32[]{:S(2)}, u32[]{:S(2)}) collective-permute-start(bf16[128,768]{1,0:T(8,128)(2,1)S(1)} %pad_maximum_fusion), channel_id=1, source_target_pairs={{0,32},{1,33},{2,34},{3,35},{4,36},{5,37},{6,38},{7,39},{8,40},{9,... | collective-permute-start | bytes 589832 | tf_op jit(solution)/shard_map/ppermute | solution.py:514

commit v5 on v4

--- a/solution.py
+++ b/solution.py
@@ -211,12 +211,12 @@
         values = jnp.concatenate([v, jnp.where(extra < 2, -1.0, 0.0)], 0).astype(bf16)
         dscores = weights.astype(f32) * mm(values, dout_more, TN)
         dround = dscores.astype(bf16)
-        dvalue = mm(dout.astype(bf16), weights, NT)
+        dvalue = mm(weights, dout.astype(bf16), NT).T
         ones = jnp.where(extra == 0, 1.0, 0.0).astype(bf16)
         dquery = mm(jnp.concatenate([k_round, ones], 0), dround)
         excess = dquery[HEAD_DIM : HEAD_DIM + 1, :]
         dquery = dquery[:HEAD_DIM, :]
-        dkey = mm(q_round, dround, NT)
+        dkey = mm(dround, q_round, NT).T
         scale_out[pl.ds(head, 1), :] = (
             jnp.sum(q_round.astype(f32) * dquery, 0, keepdims=True) - means[head] * excess
         )

time: 107 us -> 107 us (level)
  no operation moved by 1% of the time
where the time goes in v5:
time: 107 us; the launch traced here: 106 us
  blocking collectives  42 us (39%)
  Pallas kernels  25.7 us (24%)
  waiting for transfers between devices  18.7 us (17%)
  starting transfers between devices  18.2 us (17%)
    all_to_all x2, blocking collectives, exchange(): lax.all_to_all(value, BOTH, 0, 0, axis_index_groups=groups, tiled=True)  42 us
    pallas_call x1, Pallas kernels, per_device(): pl.pallas_call(window_kernel, out_shape=(jax.ShapeDtypeStruct((3840, AREA...  14.3 us
    ppermute x3, starting transfers between devices, per_device(): lax.ppermute(both[n], BOTH, shift_pairs(-steps[n][0], -steps[n][1]))  10.3 us
    all_to_all x1, starting transfers between devices, exchange(): lax.all_to_all(value, BOTH, 0, 0, axis_index_groups=groups, tiled=True)  6.97 us
    ppermute x1, waiting for transfers between devices, per_device(): from_lon = lax.ppermute(dlon, BOTH, shift_pairs(0, 1))  5.85 us
    ppermute x1, waiting for transfers between devices, per_device(): lax.ppermute(jnp.concatenate([d10, from_lon[QUAD:]], 0), BOTH, shift_pair...  5.52 us
    all_to_all x1, waiting for transfers between devices, exchange(): lax.all_to_all(value, BOTH, 0, 0, axis_index_groups=groups, tiled=True)  3.99 us
    pallas_call x1, Pallas kernels, per_device(): pl.pallas_call(bias_kernel, out_shape=(jax.ShapeDtypeStruct((HEADS, WIN,...  3.52 us
  transfers between devices with their start and end apart: 8, of which 6 were waited for; matrix products, arithmetic and copies ran while one was open for 0% of the time, Pallas kernels for 5%

profile of v5, /device:TPU:2, one launch (start us, length us, event | category | flops | bytes accessed | tf_op | source)
XLA Modules:
  0.0 106.3 jit_solution(1064815415336477761)
XLA Ops:
  0.6 0.0 copy-start.3
  0.6 0.0 copy-start.2
  0.7 0.0 copy-start.6
  0.7 0.0 copy-start.4
  0.7 0.0 copy-start.7
  0.7 0.0 copy-start.5
  0.7 2.1 %cut.1 = (bf16[128,768]{1,0:T(8,128)(2,1)}, bf16[128,768]{1,0:T(8,128)(2,1)}, bf16[128,768]{1,0:T(8,128)(2,1)}, bf16[128,768]{1,0:T(8,128)(2,1)}) custom-call(bf16[16,16,768]{2,1,0:T(8,128)(2,1)} %features_hbm.1, bf16[16,16,768]{2,1,0:T(8,128)(2,1)} %upstream_hbm.1), custom_call_target="tpu_custom_call" | custom-call | flops 2300000000 | tf_op jit(solution)/shard_map/cut/pallas_call | solution.py:413
  2.8 6.9 %collective-permute-start = (bf16[128,768]{1,0:T(8,128)(2,1)}, bf16[128,768]{1,0:T(8,128)(2,1)S(1)}, u32[]{:S(2)}, u32[]{:S(2)}) collective-permute-start(bf16[128,768]{1,0:T(8,128)(2,1)} %get-tuple-element.47), channel_id=1, source_target_pairs={{0,31},{1,0},{2,1},{3,2},{4,3},{5,4},{6,5},{7,6},{8,7},{9,8},{10,9... | collective-permute-start | bytes 589832 | tf_op jit(solution)/shard_map/ppermute | solution.py:425
  9.7 1.4 %collective-permute-start.1 = (bf16[128,768]{1,0:T(8,128)(2,1)}, bf16[128,768]{1,0:T(8,128)(2,1)S(1)}, u32[]{:S(2)}, u32[]{:S(2)}) collective-permute-start(bf16[128,768]{1,0:T(8,128)(2,1)} %get-tuple-element.48), channel_id=1, source_target_pairs={{0,224},{1,225},{2,226},{3,227},{4,228},{5,229},{6,230},{7,231},{8... | collective-permute-start | bytes 589832 | tf_op jit(solution)/shard_map/ppermute | solution.py:425
  11.1 2.0 %collective-permute-start.2 = (bf16[128,768]{1,0:T(8,128)(2,1)}, bf16[128,768]{1,0:T(8,128)(2,1)S(1)}, u32[]{:S(2)}, u32[]{:S(2)}) collective-permute-start(bf16[128,768]{1,0:T(8,128)(2,1)} %get-tuple-element.49), channel_id=1, source_target_pairs={{0,255},{1,224},{2,225},{3,226},{4,227},{5,228},{6,229},{7,230},{8... | collective-permute-start | bytes 589832 | tf_op jit(solution)/shard_map/ppermute | solution.py:425
  13.1 0.0 copy-done.3
  13.1 0.0 copy-done.2
  13.1 0.0 copy-done.6
  13.1 0.0 copy-done.4
  13.1 0.0 copy-done.7
  13.1 0.0 copy-done.5
  13.1 0.0 copy-start
  13.1 0.0 copy-start.1
  13.2 0.0 copy-start.8
  13.2 3.5 %bias.1 = (f32[24,16,512]{2,1,0:T(8,128)S(1)}, f32[256,256]{1,0:T(8,128)S(1)}, f32[24,1,256]{2,1,0:T(1,128)S(1)}, bf16[1024,512]{1,0:T(8,128)(2,1)S(1)}, bf16[10...) custom-call(s32[1]{0:T(128)} %bitcast.1.last_ref, f32[24]{0:T(128)S(1)} %copy-done.7, ...), custom_call_target="tpu_custom_call" | custom-call | flops 2300000000 | tf_op jit(solution)/shard_map/bias/pallas_call | solution.py:431
  16.7 0.0 collective-permute-done.q01
  16.7 1.0 collective-permute-done.1.q10
  17.7 0.8 collective-permute-done.2.q11
  18.6 0.0 copy-done
  18.6 0.0 copy-done.1
  18.6 0.0 copy-done.8
  18.6 14.3 %window.1 = (bf16[3840,256]{1,0:T(8,128)(2,1)S(1)}, bf16[768,256]{1,0:T(8,128)(2,1)S(1)}, bf16[64,768]{1,0:T(8,128)(2,1)S(1)}, bf16[64,768]{1,0:T(8,128)(2,1)S(1...) custom-call(s32[1]{0:T(128)} %bitcast.core_ref, ...), custom_call_target="tpu_custom_call" | custom-call | flops 19549999104 | tf_op jit(solution)/shard_map/window/pallas_call | solution.py:451
  32.9 0.1 collective-permute-start.3
  33.0 0.5 collective-permute-start.5
  33.5 1.9 %table.1.pack_ref = bf16[64,384]{1,0:T(8,128)(2,1)S(1)} custom-call(f32[24,512]{1,0:T(8,128)S(1)} %bitcast.14, bf16[1024,512]{1,0:T(8,128)(2,1)S(1)} %get-tuple-element.53.high_ref, bf16[1024,512]{1,0:T(8,128)(2,1)S(1)} %get-tuple-element.54.low_ref, f32[24,1024]{1,0:T(8,128)S(1)} %get-tuple-element.55.slope_ref, ...), custom_call_target="tpu_custom_call" | custom-call | flops 5750000128 | tf_op jit(solution)/shard_map/table/pallas_call | solution.py:482
  35.4 0.1 collective-permute-start.4
  35.5 1.5 %collective-permute-done.4.got_pack_ref = bf16[64,384]{1,0:T(8,128)(2,1)S(1)} collective-permute-done((bf16[64,384]{1,0:T(8,128)(2,1)S(1)}, bf16[64,384]{1,0:T(8,128)(2,1)S(1)}, u32[]{:S(2)}, u32[]{:S(2)}) %collective-permute-start.4) | collective-permute-done | bytes 49184 | tf_op jit(solution)/shard_map/ppermute | solution.py:492
  37.0 5.8 %collective-permute-done.5 = bf16[128,768]{1,0:T(8,128)(2,1)S(1)} collective-permute-done((bf16[128,768]{1,0:T(8,128)(2,1)S(1)}, bf16[128,768]{1,0:T(8,128)(2,1)S(1)}, u32[]{:S(2)}, u32[]{:S(2)}) %collective-permute-start.5) | collective-permute-done | bytes 196640 | tf_op jit(solution)/shard_map/ppermute | solution.py:493
  42.9 0.0 collective-permute-done.3.got_ref
  42.9 2.1 %grads.1 = bf16[16,200,384]{2,1,0:T(8,128)(2,1)S(1)} custom-call(bf16[768,256]{1,0:T(8,128)(2,1)S(1)} %get-tuple-element.51.keep_ref, bf16[3840,256]{1,0:T(8,128)(2,1)S(1)} %get-tuple-element.52.send_ref, bf16[3840,256]{1,0:T(8,128)(2,1)S(1)} %collective-permute-done.3.got_ref, bf16[64,384]{1,0:T(8,128)(2,1)S(1)} %table.1.pack_ref, ...), custom_call_target="tpu_custom_call" | custom-call | flops 2300000000 | tf_op jit(solution)/shard_map/grads/pallas_call | solution.py:495
  45.0 32.5 %all_to_all.15.in_ref = bf16[16,200,384]{2,1,0:T(8,128)(2,1)S(1)} all-to-all(bf16[16,200,384]{2,1,0:T(8,128)(2,1)S(1)} %grads.1), channel_id=1, replica_groups={{0,32,64,96,128,160,192,224,16,48,80,112,144,176,208,240},{1,33,65,97,1..., dimensions={0} | all-to-all | bytes 4915200 | tf_op jit(solution)/shard_map/all_to_all | solution.py:405
  77.5 1.0 plane.1
  78.5 7.0 %all-to-all-start.1 = ((bf16[8,32,384]{2,1,0:T(8,128)(2,1)}), bf16[8,32,384]{2,1,0:T(8,128)(2,1)S(1)}, u32[]{:S(2)}, u32[]{:S(2)}) async-start(bf16[8,32,384]{2,1,0:T(8,128)(2,1)} %plane.1), calls=%async_computation.1 | async-start | bytes 393216 | tf_op jit(solution)/shard_map/all_to_all | solution.py:405
  85.5 0.2 collective-permute-start.6
  85.7 5.5 %collective-permute-done.6 = bf16[128,768]{1,0:T(8,128)(2,1)S(1)} collective-permute-done((bf16[128,768]{1,0:T(8,128)(2,1)S(1)}, bf16[128,768]{1,0:T(8,128)(2,1)S(1)}, u32[]{:S(2)}, u32[]{:S(2)}) %collective-permute-start.6) | collective-permute-done | bytes 196640 | tf_op jit(solution)/shard_map/ppermute | solution.py:514
  91.2 4.0 %all-to-all-done.1.in_ref = bf16[8,32,384]{2,1,0:T(8,128)(2,1)S(1)} async-done(((bf16[8,32,384]{2,1,0:T(8,128)(2,1)}), bf16[8,32,384]{2,1,0:T(8,128)(2,1)S(1)}, u32[]{:S(2)}, u32[]{:S(2)}) %all-to-all-start.1) | async-done | bytes 196640 | tf_op jit(solution)/shard_map/all_to_all | solution.py:405
  95.3 0.8 maximum_maximum_fusion
  96.0 9.5 %all_to_all.16.in_ref = bf16[8,32,384]{2,1,0:T(8,128)(2,1)S(1)} all-to-all(bf16[8,32,384]{2,1,0:T(8,128)(2,1)S(1)} %column.1), channel_id=1, replica_groups={{0,32,64,96,128,160,192,224},{1,33,65,97,129,161,193,225},{2,34,66,98,1..., dimensions={0} | all-to-all | bytes 393216 | tf_op jit(solution)/shard_map/all_to_all | solution.py:405
  105.5 0.7 finish.1
  (4 shorter events, 0.1 us)
Async XLA Ops:
  0.6 12.5 %copy-start.3 = (s32[16,16]{1,0:T(8,128)S(1)}, s32[16,16]{1,0:T(8,128)}, u32[]{:S(2)}) copy-start(s32[16,16]{1,0:T(8,128)} %valid_ref.1) | copy-start | bytes 3076
  0.6 12.5 %copy-start.2 = (f32[512,24]{0,1:T(8,128)S(1)}, f32[512,24]{0,1:T(8,128)}, u32[]{:S(2)}) copy-start(f32[512,24]{0,1:T(8,128)} %param.18) | copy-start | bytes 147460
  0.7 12.5 %copy-start.6 = (f32[512]{0:T(512)S(1)}, f32[512]{0:T(512)}, u32[]{:S(2)}) copy-start(f32[512]{0:T(512)} %param.17) | copy-start | bytes 6148
  0.7 12.4 %copy-start.4 = (f32[2,512]{1,0:T(2,128)S(1)}, f32[2,512]{1,0:T(2,128)}, u32[]{:S(2)}) copy-start(f32[2,512]{1,0:T(2,128)} %inner_ref.1) | copy-start | bytes 12292
  0.7 12.4 %copy-start.7 = (f32[24]{0:T(128)S(1)}, f32[24]{0:T(128)}, u32[]{:S(2)}) copy-start(f32[24]{0:T(128)} %log_ref.1) | copy-start | bytes 292
  0.7 12.4 %copy-start.5 = (f32[768]{0:T(1024)S(1)}, f32[768]{0:T(1024)}, u32[]{:S(2)}) copy-start(f32[768]{0:T(1024)} %gain_ref.1) | copy-start | bytes 9220
  2.8 13.9 %collective-permute-start = (bf16[128,768]{1,0:T(8,128)(2,1)}, bf16[128,768]{1,0:T(8,128)(2,1)S(1)}, u32[]{:S(2)}, u32[]{:S(2)}) collective-permute-start(bf16[128,768]{1,0:T(8,128)(2,1)} %get-tuple-element.47), channel_id=1, source_target_pairs={{0,31},{1,0},{2,1},{3,2},{4,3},{5,4},{6,5},{7,6},{8,7},{9,8},{10,9... | collective-permute-start | bytes 589832 | tf_op jit(solution)/shard_map/ppermute | solution.py:425
  9.7 8.0 %collective-permute-start.1 = (bf16[128,768]{1,0:T(8,128)(2,1)}, bf16[128,768]{1,0:T(8,128)(2,1)S(1)}, u32[]{:S(2)}, u32[]{:S(2)}) collective-permute-start(bf16[128,768]{1,0:T(8,128)(2,1)} %get-tuple-element.48), channel_id=1, source_target_pairs={{0,224},{1,225},{2,226},{3,227},{4,228},{5,229},{6,230},{7,231},{8... | collective-permute-start | bytes 589832 | tf_op jit(solution)/shard_map/ppermute | solution.py:425
  11.1 7.5 %collective-permute-start.2 = (bf16[128,768]{1,0:T(8,128)(2,1)}, bf16[128,768]{1,0:T(8,128)(2,1)S(1)}, u32[]{:S(2)}, u32[]{:S(2)}) collective-permute-start(bf16[128,768]{1,0:T(8,128)(2,1)} %get-tuple-element.49), channel_id=1, source_target_pairs={{0,255},{1,224},{2,225},{3,226},{4,227},{5,228},{6,229},{7,230},{8... | collective-permute-start | bytes 589832 | tf_op jit(solution)/shard_map/ppermute | solution.py:425
  13.1 5.4 %copy-start = (bf16[768,2304]{1,0:T(8,128)(2,1)S(1)}, bf16[768,2304]{1,0:T(8,128)(2,1)}, u32[]{:S(2)}) copy-start(bf16[768,2304]{1,0:T(8,128)(2,1)} %weight_ref.1) | copy-start | bytes 10616836
  13.1 5.4 %copy-start.1 = (bf16[768,768]{1,0:T(8,128)(2,1)S(1)}, bf16[768,768]{1,0:T(8,128)(2,1)}, u32[]{:S(2)}) copy-start(bf16[768,768]{1,0:T(8,128)(2,1)} %out_weight_ref.1) | copy-start | bytes 3538948
  13.2 5.4 %copy-start.8 = (bf16[128,768]{1,0:T(8,128)(2,1)S(1)}, bf16[128,768]{1,0:T(8,128)(2,1)}, u32[]{:S(2)}) copy-start(bf16[128,768]{1,0:T(8,128)(2,1)} %get-tuple-element.46.q00) | copy-start | bytes 589828
  32.9 10.0 %collective-permute-start.3 = (bf16[3840,256]{1,0:T(8,128)(2,1)S(1)}, bf16[3840,256]{1,0:T(8,128)(2,1)S(1)}, u32[]{:S(2)}, u32[]{:S(2)}) collective-permute-start(bf16[3840,256]{1,0:T(8,128)(2,1)S(1)} %get-tuple-element.52.send_ref), channel_id=1, source_target_pairs={{0,1},{1,0},{2,3},{3,2},{4,5},{5,4},{6,7},{7,6},{8,9},{9,8},{10,11... | collective-permute-start | bytes 5898248 | tf_op jit(solution)/shard_map/ppermute | solution.py:481
  33.0 9.9 %collective-permute-start.5 = (bf16[128,768]{1,0:T(8,128)(2,1)S(1)}, bf16[128,768]{1,0:T(8,128)(2,1)S(1)}, u32[]{:S(2)}, u32[]{:S(2)}) collective-permute-start(bf16[128,768]{1,0:T(8,128)(2,1)S(1)} %get-tuple-element.59), channel_id=1, source_target_pairs={{0,1},{1,2},{2,3},{3,4},{4,5},{5,6},{6,7},{7,8},{8,9},{9,10},{10,1... | collective-permute-start | bytes 589832 | tf_op jit(solution)/shard_map/ppermute | solution.py:493
  35.4 1.6 %collective-permute-start.4 = (bf16[64,384]{1,0:T(8,128)(2,1)S(1)}, bf16[64,384]{1,0:T(8,128)(2,1)S(1)}, u32[]{:S(2)}, u32[]{:S(2)}) collective-permute-start(bf16[64,384]{1,0:T(8,128)(2,1)S(1)} %table.1.pack_ref), channel_id=1, source_target_pairs={{0,1},{1,0},{2,3},{3,2},{4,5},{5,4},{6,7},{7,6},{8,9},{9,8},{10,11... | collective-permute-start | bytes 147464 | tf_op jit(solution)/shard_map/ppermute | solution.py:492
  78.5 16.8 %all-to-all-start.1 = ((bf16[8,32,384]{2,1,0:T(8,128)(2,1)}), bf16[8,32,384]{2,1,0:T(8,128)(2,1)S(1)}, u32[]{:S(2)}, u32[]{:S(2)}) async-start(bf16[8,32,384]{2,1,0:T(8,128)(2,1)} %plane.1), calls=%async_computation.1 | async-start | bytes 393216 | tf_op jit(solution)/shard_map/all_to_all | solution.py:405
  85.5 5.7 %collective-permute-start.6 = (bf16[128,768]{1,0:T(8,128)(2,1)S(1)}, bf16[128,768]{1,0:T(8,128)(2,1)S(1)}, u32[]{:S(2)}, u32[]{:S(2)}) collective-permute-start(bf16[128,768]{1,0:T(8,128)(2,1)S(1)} %pad_maximum_fusion), channel_id=1, source_target_pairs={{0,32},{1,33},{2,34},{3,35},{4,36},{5,37},{6,38},{7,39},{8,40},{9,... | collective-permute-start | bytes 589832 | tf_op jit(solution)/shard_map/ppermute | solution.py:514
